TPU v7x, 32 devices: a whole 2x2x4 slice. The times are simulated.
32 devices in a mesh: dp: 8 (over z, core), aa: 2 (over x), ba: 2 (over y).
Axes of the slice: x: 2, y: 2, z: 4, core: 2. Of those that a mesh axis runs over, the one named last changes fastest.
Arguments:
- frames: bfloat16 [32, 1024, 512], P(('dp', 'aa', 'ba')), may hold values from -6 to 6
- segment_ids: int32 [32, 1024], P(('dp', 'aa', 'ba')), may hold values from 0 to 3, never falling along the last dimension, each value on 1 to 512 neighbouring positions
- cotangent: bfloat16 [32, 1024, 512], P(('dp', 'aa', 'ba')), may hold values from -30 to 30
- first_gain: bfloat16 [512], replicated, may hold values from 0.25 to 1.75
- first_shift: bfloat16 [512], replicated, may hold values from -2.5 to 2.5
- query_weight: bfloat16 [512, 512], P(None, ('aa', 'ba')), may hold values from -0.5 to 0.5
- query_bias: bfloat16 [512], P(('aa', 'ba')), may hold values from -2.5 to 2.5
- key_weight: bfloat16 [512, 512], P(None, ('aa', 'ba')), may hold values from -0.25 to 0.25
- value_weight: bfloat16 [512, 512], P(None, ('aa', 'ba')), may hold values from -0.25 to 0.25
- value_bias: bfloat16 [512], P(('aa', 'ba')), may hold values from -2.5 to 2.5
- out_weight: bfloat16 [512, 512], P(('aa', 'ba')), may hold values from -0.75 to 0.75
- out_bias: bfloat16 [512], replicated, may hold values from -2.5 to 2.5
- second_gain: bfloat16 [512], replicated, may hold values from 0.25 to 1.75
- second_shift: bfloat16 [512], replicated, may hold values from -2.5 to 2.5
- up_weight: bfloat16 [512, 2048], P(None, ('aa', 'ba')), may hold values from -0.25 to 0.25
- up_bias: bfloat16 [2048], P(('aa', 'ba')), may hold values from -2.5 to 2.5
- down_weight: bfloat16 [2048, 512], P(('aa', 'ba')), may hold values from -0.125 to 0.125
- down_bias: bfloat16 [512], replicated, may hold values from -2.5 to 2.5
Outputs:
- layer_output: bfloat16 [32, 1024, 512], P(('dp', 'aa', 'ba'))
- frames_delta: bfloat16 [32, 1024, 512], P(('dp', 'aa', 'ba'))
- first_gain_delta: float32 [512], replicated
- first_shift_delta: float32 [512], replicated
- query_weight_delta: float32 [512, 512], P(None, ('aa', 'ba'))
- query_bias_delta: float32 [512], P(('aa', 'ba'))
- key_weight_delta: float32 [512, 512], P(None, ('aa', 'ba'))
- value_weight_delta: float32 [512, 512], P(None, ('aa', 'ba'))
- value_bias_delta: float32 [512], P(('aa', 'ba'))
- out_weight_delta: float32 [512, 512], P(('aa', 'ba'))
- out_bias_delta: float32 [512], replicated
- second_gain_delta: float32 [512], replicated
- second_shift_delta: float32 [512], replicated
- up_weight_delta: float32 [512, 2048], P(None, ('aa', 'ba'))
- up_bias_delta: float32 [2048], P(('aa', 'ba'))
- down_weight_delta: float32 [2048, 512], P(('aa', 'ba'))
- down_bias_delta: float32 [512], replicated
Inputs may be any that keep to these rules, and one draw needn't show every extreme that they name: `segment_ids`: in each window the clip numbers never fall and every number from 0 to 3 appears; each clip covers 1 to 512 frames and one clip exactly 512.
All inputs are finite; a program needn't handle non-finite values.
Results may differ from a plain program's by a relative error of at most 0.02.
Values may be sent and summed in bfloat16 or wider, within the bound.
No kernel may reach another device: no remote copies, remote signals or barrier semaphores. Data moves between devices by JAX's collectives and lax.ppermute only.
A program may use at most 256 MiB of HBM per device.

v0:
```python
import jax
import jax.numpy as jnp
from jax import lax
from jax.sharding import PartitionSpec as P

HEAD_DIM = 64


EPSILON = 1e-05
MASKED = -1e30


def project(left, right):
    return jnp.dot(left, right, preferred_element_type=jnp.float32)


def project_back(left, right):
    return lax.dot_general(
        left, right, (((1,), (1,)), ((), ())), preferred_element_type=jnp.float32
    )


def project_over(left, right):
    return lax.dot_general(
        left, right, (((0,), (0,)), ((), ())), preferred_element_type=jnp.float32
    )


def layer_norm(values, gain, shift):
    centre = jnp.mean(values, axis=-1, keepdims=True)
    offset = values - centre
    spread = jnp.mean(offset * offset, axis=-1, keepdims=True)
    return offset * lax.rsqrt(spread + EPSILON) * gain + shift


def exact_gelu(values):
    return jax.nn.gelu(values, approximate=False)


def window_rows(stacked, row_count):
    return stacked.reshape(row_count * stacked.shape[1], stacked.shape[2])


def head_scores(query_one, key_one, labels):
    scores = project_back(query_one, key_one)
    same_clip = labels[:, None] == labels[None, :]
    return jnp.where(same_clip, scores, MASKED)


def attend(window_item):
    query_win, key_win, value_win, labels = window_item

    def one_head(head_item):
        query_one, key_one, value_one = head_item
        scores = head_scores(query_one, key_one, labels)
        row_peak = jnp.max(scores, axis=-1, keepdims=True)
        raised = jnp.exp(scores - row_peak)
        row_total = jnp.sum(raised, axis=-1, keepdims=True)
        key_weights = (raised / row_total).astype(jnp.bfloat16)
        mixed = project(key_weights, value_one)
        return (mixed.astype(jnp.bfloat16), row_peak[:, 0] + jnp.log(row_total[:, 0]))

    mixed, log_total = lax.map(
        one_head,
        (jnp.moveaxis(query_win, 1, 0), jnp.moveaxis(key_win, 1, 0), jnp.moveaxis(value_win, 1, 0)),
    )
    return (jnp.moveaxis(mixed, 0, 1), log_total)


def attend_back(window_item):
    query_win, key_win, value_win, labels, delta_mixed, log_total = window_item

    def one_head(head_item):
        query_one, key_one, value_one, delta_one, total_one = head_item
        scores = head_scores(query_one, key_one, labels)
        key_weights = jnp.exp(scores - total_one[:, None])
        delta_value = project_over(key_weights.astype(jnp.bfloat16), delta_one)
        delta_weights = project_back(delta_one, value_one)
        row_inner = jnp.sum(key_weights * delta_weights, axis=-1, keepdims=True)
        delta_scores = (key_weights * (delta_weights - row_inner)).astype(jnp.bfloat16)
        delta_query = project(delta_scores, key_one)
        delta_key = project_over(delta_scores, query_one)
        return (
            delta_query.astype(jnp.bfloat16),
            delta_key.astype(jnp.bfloat16),
            delta_value.astype(jnp.bfloat16),
        )

    delta_query, delta_key, delta_value = lax.map(
        one_head,
        (
            jnp.moveaxis(query_win, 1, 0),
            jnp.moveaxis(key_win, 1, 0),
            jnp.moveaxis(value_win, 1, 0),
            jnp.moveaxis(delta_mixed, 1, 0),
            log_total,
        ),
    )
    return (
        jnp.moveaxis(delta_query, 0, 1),
        jnp.moveaxis(delta_key, 0, 1),
        jnp.moveaxis(delta_value, 0, 1),
    )


def shards(
    frames,
    segment_ids,
    cotangent,
    first_gain,
    first_shift,
    query_weight,
    query_bias,
    key_weight,
    value_weight,
    value_bias,
    out_weight,
    out_bias,
    second_gain,
    second_shift,
    up_weight,
    up_bias,
    down_weight,
    down_bias,
):
    windows_here, length, model_width = frames.shape
    query_scale = HEAD_DIM ** (-0.5)
    gain_one = first_gain.astype(jnp.float32)
    shift_one = first_shift.astype(jnp.float32)
    gain_two = second_gain.astype(jnp.float32)
    shift_two = second_shift.astype(jnp.float32)
    frames_wide = frames.astype(jnp.float32)
    normed = layer_norm(frames_wide, gain_one, shift_one).astype(jnp.bfloat16)
    labels = segment_ids.astype(jnp.bfloat16)
    query_here, key_here, value_here, qbias_here, vbias_here, out_here = (
        lax.all_gather(query_weight, "ba", axis=1, tiled=True),
        lax.all_gather(key_weight, "ba", axis=1, tiled=True),
        lax.all_gather(value_weight, "ba", axis=1, tiled=True),
        lax.all_gather(query_bias, "ba", axis=0, tiled=True),
        lax.all_gather(value_bias, "ba", axis=0, tiled=True),
        lax.all_gather(out_weight, "ba", axis=0, tiled=True),
    )
    up_here, upbias_here, down_here = (up_weight, up_bias, down_weight)
    normed_all, labels_all = (
        lax.all_gather(normed, "aa", axis=0, tiled=True),
        lax.all_gather(labels, "aa", axis=0, tiled=True),
    )
    head_width = query_here.shape[1]
    heads_here = head_width // HEAD_DIM
    attn_count = normed_all.shape[0]
    joint_weight = jnp.concatenate([query_here, key_here, value_here], axis=1)
    normed_flat = normed_all.reshape(attn_count * length, model_width)
    joint_linear = project(normed_flat, joint_weight)
    query_all = (
        query_scale * (joint_linear[:, :head_width] + qbias_here.astype(jnp.float32))
    ).astype(jnp.bfloat16)
    key_all = joint_linear[:, head_width : 2 * head_width].astype(jnp.bfloat16)
    value_all = (joint_linear[:, 2 * head_width :] + vbias_here.astype(jnp.float32)).astype(
        jnp.bfloat16
    )
    head_shape = (attn_count, length, heads_here, HEAD_DIM)
    query_heads = query_all.reshape(head_shape)
    key_heads = key_all.reshape(head_shape)
    value_heads = value_all.reshape(head_shape)
    mixed_heads, log_total = lax.map(attend, (query_heads, key_heads, value_heads, labels_all))
    mixed_flat = mixed_heads.reshape(attn_count * length, head_width)
    mixed_rows = mixed_heads.reshape(attn_count, length, head_width)
    row_count = lax.axis_size("aa") * windows_here
    branch = lax.psum_scatter(
        project(window_rows(mixed_rows, row_count), out_here).reshape(
            row_count, length, model_width
        ),
        "aa",
        scatter_dimension=0,
        tiled=True,
    )
    inner_sum = frames_wide + branch + out_bias.astype(jnp.float32)
    normed_two = layer_norm(inner_sum, gain_two, shift_two).astype(jnp.bfloat16)
    feed_normed = lax.all_gather(normed_two, ("aa", "ba"), axis=0, tiled=True)
    feed_count = feed_normed.shape[0]
    feed_flat = feed_normed.reshape(feed_count * length, model_width)
    up_linear = project(feed_flat, up_here) + upbias_here.astype(jnp.float32)
    activated_wide, gelu_back = jax.vjp(exact_gelu, up_linear)
    activated = activated_wide.astype(jnp.bfloat16)
    activated_rows = activated.reshape(feed_count, length, -1)
    row_count = windows_here * lax.axis_size(("aa", "ba"))
    feed_output = lax.psum_scatter(
        project(window_rows(activated_rows, row_count), down_here)
        .reshape(row_count, length, model_width)
        .astype(jnp.bfloat16),
        ("aa", "ba"),
        scatter_dimension=0,
        tiled=True,
    ).astype(jnp.float32)
    layer_output = (inner_sum + feed_output + down_bias.astype(jnp.float32)).astype(jnp.bfloat16)
    cot_all = lax.all_gather(cotangent, ("aa", "ba"), axis=0, tiled=True)
    cot_flat = cot_all.reshape(feed_count * length, model_width)
    down_change = project_over(activated, cot_flat)
    delta_active = project_back(cot_flat, down_here)
    delta_up = gelu_back(delta_active)[0].astype(jnp.bfloat16)
    up_change = project_over(feed_flat, delta_up)
    upbias_change = jnp.sum(delta_up.astype(jnp.float32), axis=0)
    delta_up_rows = delta_up.reshape(feed_count, length, -1)
    row_count = lax.axis_size(("aa", "ba")) * windows_here
    delta_two = lax.psum_scatter(
        project_back(window_rows(delta_up_rows, row_count), up_here).reshape(
            row_count, length, model_width
        ),
        ("aa", "ba"),
        scatter_dimension=0,
        tiled=True,
    )
    unused, norm_two_back = jax.vjp(layer_norm, inner_sum, gain_two, shift_two)
    delta_inner_norm, gain_two_change, shift_two_change = norm_two_back(delta_two)
    cot_wide = cotangent.astype(jnp.float32)
    delta_inner = cot_wide + delta_inner_norm
    delta_branch = delta_inner.astype(jnp.bfloat16)
    outbias_change = jnp.sum(delta_branch.astype(jnp.float32), axis=(0, 1))
    downbias_change = jnp.sum(cot_wide, axis=(0, 1))
    branch_all = lax.all_gather(delta_branch, "aa", axis=0, tiled=True)
    branch_flat = branch_all.reshape(attn_count * length, model_width)
    out_change = project_over(mixed_flat, branch_flat)
    delta_mixed = project_back(branch_flat, out_here).astype(jnp.bfloat16).reshape(head_shape)
    delta_query, delta_key, delta_value = lax.map(
        attend_back, (query_heads, key_heads, value_heads, labels_all, delta_mixed, log_total)
    )
    delta_query = delta_query * query_scale
    delta_joint = jnp.concatenate(
        [
            delta_query.reshape(-1, head_width),
            delta_key.reshape(-1, head_width),
            delta_value.reshape(-1, head_width),
        ],
        axis=1,
    )
    joint_change = project_over(normed_flat, delta_joint)
    query_change = joint_change[:, :head_width]
    key_change = joint_change[:, head_width : 2 * head_width]
    value_change = joint_change[:, 2 * head_width :]
    joint_sums = jnp.sum(delta_joint.astype(jnp.float32), axis=0)
    qbias_change = joint_sums[:head_width]
    vbias_change = joint_sums[2 * head_width :]
    delta_joint_rows = delta_joint.reshape(attn_count, length, 3 * head_width)
    row_count = windows_here * lax.axis_size("aa")
    delta_one = lax.psum_scatter(
        project_back(window_rows(delta_joint_rows, row_count), joint_weight)
        .reshape(row_count, length, model_width)
        .astype(jnp.bfloat16),
        "aa",
        scatter_dimension=0,
        tiled=True,
    ).astype(jnp.float32)
    unused_one, norm_one_back = jax.vjp(layer_norm, frames_wide, gain_one, shift_one)
    delta_frames, gain_one_change, shift_one_change = norm_one_back(delta_one)
    frames_delta = (delta_inner + delta_frames).astype(jnp.bfloat16)
    query_change, qbias_change, key_change, value_change, vbias_change, out_change = (
        lax.psum_scatter(
            query_change.astype(jnp.bfloat16), "ba", scatter_dimension=1, tiled=True
        ).astype(jnp.float32),
        lax.psum_scatter(
            qbias_change.astype(jnp.bfloat16), "ba", scatter_dimension=0, tiled=True
        ).astype(jnp.float32),
        lax.psum_scatter(
            key_change.astype(jnp.bfloat16), "ba", scatter_dimension=1, tiled=True
        ).astype(jnp.float32),
        lax.psum_scatter(
            value_change.astype(jnp.bfloat16), "ba", scatter_dimension=1, tiled=True
        ).astype(jnp.float32),
        lax.psum_scatter(
            vbias_change.astype(jnp.bfloat16), "ba", scatter_dimension=0, tiled=True
        ).astype(jnp.float32),
        lax.psum_scatter(
            out_change.astype(jnp.bfloat16), "ba", scatter_dimension=0, tiled=True
        ).astype(jnp.float32),
    )
    (
        query_change,
        qbias_change,
        key_change,
        value_change,
        vbias_change,
        out_change,
        up_change,
        upbias_change,
        down_change,
    ) = (
        lax.psum(query_change.astype(jnp.bfloat16), "dp").astype(jnp.float32),
        lax.psum(qbias_change.astype(jnp.bfloat16), "dp").astype(jnp.float32),
        lax.psum(key_change.astype(jnp.bfloat16), "dp").astype(jnp.float32),
        lax.psum(value_change.astype(jnp.bfloat16), "dp").astype(jnp.float32),
        lax.psum(vbias_change.astype(jnp.bfloat16), "dp").astype(jnp.float32),
        lax.psum(out_change.astype(jnp.bfloat16), "dp").astype(jnp.float32),
        lax.psum(up_change.astype(jnp.bfloat16), "dp").astype(jnp.float32),
        lax.psum(upbias_change.astype(jnp.bfloat16), "dp").astype(jnp.float32),
        lax.psum(down_change.astype(jnp.bfloat16), "dp").astype(jnp.float32),
    )
    (
        gain_one_change,
        shift_one_change,
        gain_two_change,
        shift_two_change,
        outbias_change,
        downbias_change,
    ) = lax.psum(
        (
            gain_one_change,
            shift_one_change,
            gain_two_change,
            shift_two_change,
            outbias_change,
            downbias_change,
        ),
        ("dp", "aa", "ba"),
    )
    return (
        layer_output,
        frames_delta,
        gain_one_change,
        shift_one_change,
        query_change,
        qbias_change,
        key_change,
        value_change,
        vbias_change,
        out_change,
        outbias_change,
        gain_two_change,
        shift_two_change,
        up_change,
        upbias_change,
        down_change,
        downbias_change,
    )


def solution(mesh):
    placed = (
        P(("dp", "aa", "ba"), None, None),
        P(("dp", "aa", "ba"), None),
        P(("dp", "aa", "ba"), None, None),
        P(),
        P(),
        P(None, ("aa", "ba")),
        P(("aa", "ba")),
        P(None, ("aa", "ba")),
        P(None, ("aa", "ba")),
        P(("aa", "ba")),
        P(("aa", "ba"), None),
        P(),
        P(),
        P(),
        P(None, ("aa", "ba")),
        P(("aa", "ba")),
        P(("aa", "ba"), None),
        P(),
    )
    return jax.shard_map(
        shards,
        mesh=mesh,
        in_specs=placed,
        out_specs=(
            P(("dp", "aa", "ba"), None, None),
            P(("dp", "aa", "ba"), None, None),
            P(),
            P(),
            P(None, ("aa", "ba")),
            P(("aa", "ba")),
            P(None, ("aa", "ba")),
            P(None, ("aa", "ba")),
            P(("aa", "ba")),
            P(("aa", "ba"), None),
            P(),
            P(),
            P(),
            P(None, ("aa", "ba")),
            P(("aa", "ba")),
            P(("aa", "ba"), None),
            P(),
        ),
        check_vma=False,
    )
```

profile of v0, /device:TPU:0, one launch (start us, length us, event | category | flops | bytes accessed | tf_op | source)
XLA Modules:
  0.0 816.7 jit_solution(15029289896997955831)
XLA Ops:
  16.0 5.1 all-gather
  29.7 6.5 all_gather.40
  36.2 7.1 all_gather.34
  43.3 6.1 all_gather.35
  49.5 5.7 all_gather.36
  77.6 40.9 %while.53 = (s32[]{:T(128)}, bf16[2,1024,4,64]{1,3,2,0:T(8,128)(2,1)}, f32[2,4,1024]{2,1,0:T(4,128)S(1)}, bf16[2,1024,4,64]{3,1,2,0:T(8,128)(2,1)}, bf16[2,1024,...) while((s32[]{:T(128)}, ...), condition=%wide.region_7.8_spmd, body=%wide.region_2.7_spmd.sunk | while | flops 281082880 | bytes 17785152 | solution.py:165
  81.7 15.6 %while.56 = (s32[]{:T(128)}, bf16[4,1024,64]{1,2,0:T(8,128)(2,1)S(1)}, f32[4,1024]{1,0:T(4,128)S(1)}, bf16[1024]{0:T(1024)(128)(2,1)S(1)}, bf16[4,1024,64]{2,1,0...) while((s32[]{:T(128)}, ...), condition=%wide.region_6.6_spmd, body=%wide.region_3.5_spmd.sunk | while | flops 281082880 | bytes 13553769 | solution.py:63
  102.1 15.6 %while.56 = (s32[]{:T(128)}, bf16[4,1024,64]{1,2,0:T(8,128)(2,1)S(1)}, f32[4,1024]{1,0:T(4,128)S(1)}, bf16[1024]{0:T(1024)(128)(2,1)S(1)}, bf16[4,1024,64]{2,1,0...) while((s32[]{:T(128)}, ...), condition=%wide.region_6.6_spmd, body=%wide.region_3.5_spmd.sunk | while | flops 281082880 | bytes 13553769 | solution.py:63
  123.1 55.1 %reduce-scatter.19.cloned.1.call-done = f32[1,1024,512]{2,1,0:T(8,128)} async-done(((f32[2,1024,512]{2,1,0:T(8,128)}), f32[1,1024,512]{2,1,0:T(8,128)}) %reduce-scatter.19.cloned.1.call-update) | async-done | bytes 2097168 | tf_op jit(solution)/shard_map/reduce_scatter | solution.py:169
  182.9 52.2 %all-gather.10.cloned.1.call-done = bf16[4,1024,512]{2,1,0:T(8,128)(2,1)} async-done(((bf16[1,1024,512]{2,1,0:T(8,128)(2,1)}), bf16[4,1024,512]{2,1,0:T(8,128)(2,1)}) %all-gather.10.cloned.1.call-update) | async-done | bytes 4194320 | tf_op jit(solution)/shard_map/all_gather | solution.py:179
  235.2 7.8 fusion.94
  242.9 46.8 %all-gather.12.cloned.1.call-done = bf16[4,1024,512]{2,1,0:T(8,128)(2,1)} async-done(((bf16[1,1024,512]{2,1,0:T(8,128)(2,1)}), bf16[4,1024,512]{2,1,0:T(8,128)(2,1)}) %all-gather.12.cloned.1.call-update) | async-done | bytes 4194320 | tf_op jit(solution)/shard_map/all_gather | solution.py:196
  289.7 25.3 %fusion.85 = (bf16[512]{0:T(512)(128)(2,1)}, bf16[4096,512]{1,0:T(8,128)(2,1)S(1)}, f32[4096,512]{1,0:T(8,128)}) fusion(f32[4096,512]{1,0:T(8,128)} %fusion.94, f32[512]{0:T(512)S(1)} %convert_element_type.180, bf16[4096,512]{1,0:T(8,128)(2,1)} %bitcast.261, bf16[512,512]{1,0:T(8,128)(2,1)S(1)} %copy-done), kind=kOutput, calls=%fused_computation.159 | convolution fusion | flops 2302672384 | bytes 25693184 | tf_op jit(solution)/shard_map/dot_general | solution.py:18
  315.0 5.8 fusion.95
  321.0 10.1 %multiply_convert_fusion.1 = bf16[4096,512]{1,0:T(8,128)(2,1)} fusion(f32[4096,512]{1,0:T(8,128)} %get-tuple-element.368, f32[4096,512]{1,0:T(8,128)} %fusion.94, f32[512]{0:T(512)S(1)} %convert_element_type.180), kind=kLoop, calls=%fused_computation.80 | loop fusion | flops 8388608 | bytes 20973568 | tf_op jit(solution)/shard_map/convert_element_type | solution.py:184
  331.1 6.5 convolution_convert_fusion.2
  338.3 69.1 %reduce-scatter.33.cloned.1.call-done = f32[1,1024,512]{2,1,0:T(8,128)} async-done(((f32[4,1024,512]{2,1,0:T(8,128)}), f32[1,1024,512]{2,1,0:T(8,128)}) %reduce-scatter.33.cloned.1.call-update) | async-done | bytes 2097168
  410.4 52.6 %reduce-scatter.31.cloned.1.call-done = bf16[1,1024,512]{2,1,0:T(8,128)(2,1)} async-done(((bf16[4,1024,512]{2,1,0:T(8,128)(2,1)}), bf16[1,1024,512]{2,1,0:T(8,128)(2,1)}) %reduce-scatter.31.cloned.1.call-update) | async-done | bytes 1048592
  469.7 33.2 %all-gather.14.cloned.1.call-done = bf16[2,1024,512]{2,1,0:T(8,128)(2,1)} async-done(((bf16[1,1024,512]{2,1,0:T(8,128)(2,1)}), bf16[2,1024,512]{2,1,0:T(8,128)(2,1)}) %all-gather.14.cloned.1.call-update) | async-done | bytes 2097168 | tf_op jit(solution)/shard_map/all_gather | solution.py:220
  510.4 86.4 %while.55 = (s32[]{:T(128)}, bf16[2,1024,4,64]{1,3,2,0:T(8,128)(2,1)}, bf16[2,1024,4,64]{1,3,2,0:T(8,128)(2,1)}, bf16[2,1024,4,64]{1,3,2,0:T(8,128)(2,1)}, bf16[...) while((s32[]{:T(128)}, ...), condition=%wide.region_19.20_spmd, body=%wide.region_15.19_spmd.sunk | while | flops 687012864 | bytes 50544052 | solution.py:224
  514.8 33.0 %while.57 = (s32[]{:T(128)}, bf16[4,1024,64]{1,2,0:T(8,128)(2,1)}, bf16[4,1024,64]{1,2,0:T(8,128)(2,1)}, bf16[4,1024,64]{1,2,0:T(8,128)(2,1)}, bf16[1024]{0:T(10...) while((s32[]{:T(128)}, bf16[4,1024,64]{1,2,0:T(8,128)(2,1)}, ...), condition=%wide.region_18.18_spmd, body=%wide.region_16.17_spmd.sunk | while | flops 687012864 | bytes 33729656 | solution.py:89
  557.9 33.0 %while.57 = (s32[]{:T(128)}, bf16[4,1024,64]{1,2,0:T(8,128)(2,1)}, bf16[4,1024,64]{1,2,0:T(8,128)(2,1)}, bf16[4,1024,64]{1,2,0:T(8,128)(2,1)}, bf16[1024]{0:T(10...) while((s32[]{:T(128)}, bf16[4,1024,64]{1,2,0:T(8,128)(2,1)}, ...), condition=%wide.region_18.18_spmd, body=%wide.region_16.17_spmd.sunk | while | flops 687012864 | bytes 33729656 | solution.py:89
  609.7 6.8 convolution_convert_fusion.7
  618.0 6.7 convolution_convert_fusion.6
  626.4 6.3 reduce-scatter.27.cloned.1.call-done
  634.4 12.7 %reduce-scatter.25.cloned.1.call-done = bf16[128,512]{1,0:T(8,128)(2,1)} async-done(((bf16[256,512]{1,0:T(8,128)(2,1)}), bf16[128,512]{1,0:T(8,128)(2,1)}) %reduce-scatter.25.cloned.1.call-update) | async-done | bytes 131088
  648.8 12.9 %reduce-scatter.23.cloned.1.call-done = bf16[128,512]{1,0:T(8,128)(2,1)} async-done(((bf16[256,512]{1,0:T(8,128)(2,1)}), bf16[128,512]{1,0:T(8,128)(2,1)}) %reduce-scatter.23.cloned.1.call-update) | async-done | bytes 131088 | tf_op jit(solution)/shard_map/reduce_scatter | solution.py:272
  670.1 4.9 all-reduce.7
  675.2 16.0 %all-reduce.5 = (bf16[128]{0:T(256)(128)(2,1)S(1)}, bf16[128]{0:T(256)(128)(2,1)S(1)}, bf16[512]{0:T(512)(128)(2,1)S(1)}) all-reduce(bf16[128]{0:T(256)(128)(2,1)S(1)} %dynamic-slice.5, bf16[128]{0:T(256)(128)(2,1)S(1)} %dynamic-slice.7, bf16[512]{0:T(512)(128)(2,1)S(1)} %copy-done.43), channel_id=1, replica_groups=mesh['dp'=8,'aa'=2,'ba'=2] {'dp'}, use_global_device_ids=true, to_apply=%region_31.32 | all-reduce | flops 768 | bytes 3072 | tf_op jit(solution)/shard_map/psum | solution.py:288
  692.8 35.4 %all-reduce.10.cloned.1.call-done = (bf16[512,128]{1,0:T(8,128)(2,1)}, bf16[512,128]{1,0:T(8,128)(2,1)}, bf16[512,128]{1,0:T(8,128)(2,1)}, bf16[128,512]{1,0:T(8...) async-done(((bf16[512,128]{1,0:T(8,128)(2,1)}, bf16[512,128]{1,0:T(8,128)(2,1)}, bf16[512,128]{1,0:T(8,128)(2,1)}, bf16[128,512]{1,0:T(8,128)(2,1)}, ...) | async-done | bytes 1572880 | tf_op jit(solution)/shard_map/psum | solution.py:287
  739.1 23.1 %reduce-scatter.21.cloned.1.call-done = bf16[1,1024,512]{2,1,0:T(8,128)(2,1)} async-done(((bf16[2,1024,512]{2,1,0:T(8,128)(2,1)}), bf16[1,1024,512]{2,1,0:T(8,128)(2,1)}) %reduce-scatter.21.cloned.1.call-update) | async-done | bytes 1048592 | tf_op jit(solution)/shard_map/reduce_scatter | solution.py:245
  770.2 39.5 %all-reduce.4 = (f32[512]{0:T(512)}, f32[512]{0:T(512)}, f32[512]{0:T(512)}, f32[512]{0:T(512)}, f32[512]{0:T(512)}, /*index=5*/f32[512]{0:T(512)}) all-reduce(f32[512]{0:T(512)S(1)} %get-tuple-element.276, f32[512]{0:T(512)S(1)} %get-tuple-element.279, ...), channel_id=1, replica_groups=mesh['dp'=8,'aa'=2,'ba'=2] {'dp','aa','ba'}, use_global_device_ids=true, to_apply=%region_24.25 | all-reduce | flops 3072 | bytes 24576 | tf_op jit(solution)/shard_map/psum | solution.py:304
  (347 shorter events, 240.7 us)
Async XLA Ops:
  7.2 282.5 %copy-start = (bf16[512,512]{1,0:T(8,128)(2,1)S(1)}, bf16[512,512]{1,0:T(8,128)(2,1)}, u32[]{:S(2)}) copy-start(bf16[512,512]{1,0:T(8,128)(2,1)} %param.42) | copy-start | bytes 1572868
  7.2 13.9 %copy-start.45 = (bf16[128]{0:T(256)(128)(2,1)S(1)}, bf16[128]{0:T(256)(128)(2,1)}, u32[]{:S(2)}) copy-start(bf16[128]{0:T(256)(128)(2,1)} %param.35) | copy-start | bytes 772
  7.2 18.1 %copy-start.37 = (s32[1,1024]{1,0:T(1,128)S(1)}, s32[1,1024]{1,0:T(1,128)}, u32[]{:S(2)}) copy-start(s32[1,1024]{1,0:T(1,128)} %param.27) | copy-start | bytes 12292
  7.2 22.5 %copy-start.22 = (bf16[128,512]{1,0:T(8,128)(2,1)S(1)}, bf16[128,512]{1,0:T(8,128)(2,1)}, u32[]{:S(2)}) copy-start(bf16[128,512]{1,0:T(8,128)(2,1)} %param.36) | copy-start | bytes 393220
  7.2 29.0 %copy-start.23 = (bf16[512,128]{1,0:T(8,128)(2,1)S(1)}, bf16[512,128]{1,0:T(8,128)(2,1)}, u32[]{:S(2)}) copy-start(bf16[512,128]{1,0:T(8,128)(2,1)} %param.31) | copy-start | bytes 393220
  7.3 36.1 %copy-start.24 = (bf16[512,128]{1,0:T(8,128)(2,1)S(1)}, bf16[512,128]{1,0:T(8,128)(2,1)}, u32[]{:S(2)}) copy-start(bf16[512,128]{1,0:T(8,128)(2,1)} %param.33) | copy-start | bytes 393220
  7.3 42.2 %copy-start.25 = (bf16[512,128]{1,0:T(8,128)(2,1)S(1)}, bf16[512,128]{1,0:T(8,128)(2,1)}, u32[]{:S(2)}) copy-start(bf16[512,128]{1,0:T(8,128)(2,1)} %param.34) | copy-start | bytes 393220
  7.3 48.0 %all-gather.8.cloned.1.call-start = ((), (), s32[]{:S(2)}) async-start(), calls=%async_computation.8 | async-start | bytes 3145728 | tf_op jit(solution)/shard_map/all_gather | solution.py:145
  15.9 162.3 %reduce-scatter.19.cloned.1.call-start = ((), (), s32[]{:S(2)}) async-start(), calls=%async_computation.9 | async-start | bytes 6291456 | tf_op jit(solution)/shard_map/reduce_scatter | solution.py:169
  77.6 40.9 %copy-start.16 = (bf16[256,512]{1,0:T(8,128)(2,1)S(1)}, bf16[256,512]{1,0:T(8,128)(2,1)}, u32[]{:S(2)}) copy-start(bf16[256,512]{1,0:T(8,128)(2,1)} %all_gather.40) | copy-start | bytes 786436
  122.5 112.6 %all-gather.10.cloned.1.call-start = ((), (), s32[]{:S(2)}) async-start(), calls=%async_computation.10 | async-start | bytes 5242880 | tf_op jit(solution)/shard_map/all_gather | solution.py:179
  180.4 54.7 %copy-start.18 = (bf16[512,512]{1,0:T(8,128)(2,1)S(1)}, bf16[512,512]{1,0:T(8,128)(2,1)}, u32[]{:S(2)}) copy-start(bf16[512,512]{1,0:T(8,128)(2,1)} %param.40) | copy-start | bytes 1572868
  182.3 107.4 %all-gather.12.cloned.1.call-start = ((), (), s32[]{:S(2)}) async-start(), calls=%async_computation.11 | async-start | bytes 5242880 | tf_op jit(solution)/shard_map/all_gather | solution.py:196
  182.9 224.5 %reduce-scatter.33.cloned.1.call-start = ((), (), s32[]{:S(2)}) async-start(), calls=%async_computation.19 | async-start | bytes 10485760
  320.8 142.1 %reduce-scatter.31.cloned.1.call-start = ((), (), s32[]{:S(2)}) async-start(), calls=%async_computation.18 | async-start | bytes 5242880
  337.7 165.2 %all-gather.14.cloned.1.call-start = ((), (), s32[]{:S(2)}) async-start(), calls=%async_computation.12 | async-start | bytes 3145728 | tf_op jit(solution)/shard_map/all_gather | solution.py:220
  466.3 38.9 %copy-start.30 = (f32[1024]{0:T(1024)}, f32[1024]{0:T(1024)S(1)}, u32[]{:S(2)}) copy-start(f32[1024]{0:T(1024)S(1)} %negate_multiply_fusion.2) | copy-start | bytes 12292
  469.6 155.1 %reduce-scatter.29.cloned.1.call-start = ((), (), s32[]{:S(2)}) async-start(), calls=%async_computation.17 | async-start | bytes 393216
  606.4 26.3 %reduce-scatter.27.cloned.1.call-start = ((), (), s32[]{:S(2)}) async-start(), calls=%async_computation.16 | async-start | bytes 393216
  607.3 39.8 %reduce-scatter.25.cloned.1.call-start = ((), (), s32[]{:S(2)}) async-start(), calls=%async_computation.15 | async-start | bytes 393216
  609.7 52.1 %reduce-scatter.23.cloned.1.call-start = ((), (), s32[]{:S(2)}) async-start(), calls=%async_computation.14 | async-start | bytes 393216 | tf_op jit(solution)/shard_map/reduce_scatter | solution.py:272
  618.0 44.1 %copy-start.11 = (bf16[2048,768]{0,1:T(8,128)(2,1)S(1)}, bf16[2048,768]{0,1:T(8,128)(2,1)}, u32[]{:S(2)}) copy-start(bf16[2048,768]{0,1:T(8,128)(2,1)} %copy-done.10) | copy-start | bytes 9437188
  618.0 110.3 %all-reduce.10.cloned.1.call-start = ((), (), s32[]{:S(2)}) async-start(), calls=%async_computation.20 | async-start | bytes 3145728 | tf_op jit(solution)/shard_map/psum | solution.py:287
  661.7 100.4 %reduce-scatter.21.cloned.1.call-start = ((), (), s32[]{:S(2)}) async-start(), calls=%async_computation.13 | async-start | bytes 3145728 | tf_op jit(solution)/shard_map/reduce_scatter | solution.py:245
  666.4 95.8 %copy-start.4 = (bf16[1,1024,512]{2,1,0:T(8,128)(2,1)S(1)}, bf16[1,1024,512]{2,1,0:T(8,128)(2,1)}, u32[]{:S(2)}) copy-start(bf16[1,1024,512]{2,1,0:T(8,128)(2,1)} %param.26) | copy-start | bytes 3145732
  666.4 95.7 %copy-start.21 = (f32[1024]{0:T(1024)S(1)}, f32[1024]{0:T(1024)}, u32[]{:S(2)}) copy-start(f32[1024]{0:T(1024)} %copy-done.20) | copy-start | bytes 12292
  666.5 95.7 %copy-start.29 = (f32[512]{0:T(512)S(1)}, f32[512]{0:T(512)}, u32[]{:S(2)}) copy-start(f32[512]{0:T(512)} %copy-done.28) | copy-start | bytes 6148
  670.1 94.3 %copy-start.33 = (f32[1024]{0:T(1024)S(1)}, f32[1024]{0:T(1024)}, u32[]{:S(2)}) copy-start(f32[1024]{0:T(1024)} %copy-done.32) | copy-start | bytes 12292
  670.1 94.3 %copy-start.27 = (f32[1024]{0:T(1024)S(1)}, f32[1024]{0:T(1024)}, u32[]{:S(2)}) copy-start(f32[1024]{0:T(1024)} %copy-done.26) | copy-start | bytes 12292
  729.9 37.1 %copy-start.8 = (bf16[1,1024,512]{2,1,0:T(8,128)(2,1)S(1)}, bf16[1,1024,512]{2,1,0:T(8,128)(2,1)}, u32[]{:S(2)}) copy-start(bf16[1,1024,512]{2,1,0:T(8,128)(2,1)} %param.28) | copy-start | bytes 3145732
  729.9 37.1 %copy-start.31 = (f32[1024]{0:T(1024)S(1)}, f32[1024]{0:T(1024)}, u32[]{:S(2)}) copy-start(f32[1024]{0:T(1024)} %copy-done.30) | copy-start | bytes 12292
  764.4 45.4 %copy-start.1 = (bf16[512,512]{1,0:T(8,128)(2,1)S(1)}, bf16[512,512]{1,0:T(8,128)(2,1)}, u32[]{:S(2)}) copy-start(bf16[512,512]{1,0:T(8,128)(2,1)} %param.42) | copy-start | bytes 1572868
  (30 other events, 116.1 us)
Sparse Core Ops, SparseCore 0:
  16.0 35.8 all-gather.7
  122.7 55.5 reduce-scatter.18
  182.4 52.6 all-gather.9
  237.0 52.6 all-gather.11
  320.9 86.4 reduce-scatter.32
  410.2 52.6 reduce-scatter.30
  469.8 33.0 all-gather.13
  606.5 11.6 reduce-scatter.28
  621.1 11.6 reduce-scatter.26
  635.5 11.6 reduce-scatter.24
  650.0 11.6 reduce-scatter.22
  665.8 62.3 all-reduce.9
  730.6 31.5 reduce-scatter.20
where the time goes:
time: 828 us; the launch traced here: 817 us
  waiting for transfers between devices  400 us (48%)
  matrix products  157 us (19%)
  blocking collectives  99.6 us (12%)
  local copies, waits for them, and re-layouts  72.1 us (9%)
  other arithmetic  70.3 us (8%)
  between operations  15.8 us (2%)
    unnamed x18, waiting for transfers between devices  141 us
    dot_general x28, matrix products, project_back(): lax.dot_general(left, right, (((1,), (1,)), ((), ())), preferred_element_...  65.7 us
    reduce_scatter x1, waiting for transfers between devices, shards(): lax.psum_scatter(project(window_rows(mixed_rows, row_count), out_here).re...  55.1 us
    all_gather x1, waiting for transfers between devices, shards(): feed_normed = lax.all_gather(normed_two, ('aa', 'ba'), axis=0, tiled=True)  52.2 us
    dot_general x20, matrix products, project(): return jnp.dot(left, right, preferred_element_type=jnp.float32)  48.7 us
    all_gather x1, waiting for transfers between devices, shards(): cot_all = lax.all_gather(cotangent, ('aa', 'ba'), axis=0, tiled=True)  46.8 us
    dot_general x20, matrix products, project_over(): lax.dot_general(left, right, (((0,), (0,)), ((), ())), preferred_element_...  42.1 us
    psum x1, blocking collectives, shards(): lax.psum((gain_one_change, shift_one_change, gain_two_change, shift_two_c...  39.5 us
  transfers between devices with their start and end apart: 13, of which 11 were waited for; matrix products, arithmetic and copies ran while one was open for 9% of the time, Pallas kernels for 0%

commit v1 on v0

v1 whole, which is shorter than its diff:
```python
import functools

import jax
import jax.numpy as jnp
from jax import lax
from jax.experimental import pallas as pl
from jax.experimental.pallas import tpu as pltpu
from jax.sharding import PartitionSpec as P

HEAD_DIM = 64
PAIR = 2 * HEAD_DIM
BLOCK = 128
ROWS = 256
EPSILON = 1e-05
MASKED = -1e30
SPANS = (2, 3, 4, 5, 6, 8)

F32 = jnp.float32
BF16 = jnp.bfloat16
NN = (((1,), (0,)), ((), ()))
NT = (((1,), (1,)), ((), ()))
TN = (((0,), (0,)), ((), ()))
VMEM = pl.BlockSpec(memory_space=pltpu.VMEM)
SMEM = pl.BlockSpec(memory_space=pltpu.SMEM)
LIMIT = 60 * 1024 * 1024


def dot(left, right, dims=NN):
    return lax.dot_general(left, right, dims, preferred_element_type=F32)


def call(body, out_shape, in_specs, scratch, flops, *args):
    moved = sum(a.size * a.dtype.itemsize for a in args)
    moved += sum(o.size * o.dtype.itemsize for o in out_shape)
    return pl.pallas_call(
        body,
        out_shape=out_shape,
        in_specs=in_specs,
        out_specs=[VMEM] * len(out_shape),
        scratch_shapes=scratch,
        compiler_params=pltpu.CompilerParams(vmem_limit_bytes=LIMIT),
        cost_estimate=pl.CostEstimate(flops=int(flops), bytes_accessed=int(moved), transcendentals=0),
    )(*args)


def shape(dims, dtype):
    return jax.ShapeDtypeStruct(dims, dtype)


def centred(values):
    centre = jnp.mean(values, axis=-1, keepdims=True)
    offset = values - centre
    spread = jnp.mean(offset * offset, axis=-1, keepdims=True)
    scale = lax.rsqrt(spread + EPSILON)
    return offset * scale, scale


def lane_of(dims):
    return lax.broadcasted_iota(jnp.int32, dims, 1)


def key_range(lab_s, at, blocks):
    first = lab_s[0, at * BLOCK]
    last = lab_s[0, at * BLOCK + BLOCK - 1]
    low = jnp.int32(0)
    high = jnp.int32(blocks)
    for b in range(blocks):
        low += (lab_s[0, b * BLOCK + BLOCK - 1] < first).astype(jnp.int32)
        high -= (lab_s[0, b * BLOCK] > last).astype(jnp.int32)
    return low, high - low


def each_query_block(lab_s, blocks, body):
    spans = [s for s in SPANS if s < blocks] + [blocks]

    def step(at, carry):
        low, count = key_range(lab_s, at, blocks)
        under = 0
        for span in spans:
            base = jnp.minimum(low, blocks - span)

            @pl.when((count > under) & (count <= span))
            def _():
                body(at, base, span)

            under = span
        return carry

    lax.fori_loop(0, blocks, step, 0)


def fill_heads(rows_at, wide, masked_to, pair):
    lane = lane_of(wide.shape)
    zero = jnp.zeros_like(wide)
    for part in range(wide.shape[0] // BLOCK):
        piece = wide[part * BLOCK : (part + 1) * BLOCK]
        for head in range(2):
            keep = (lane[:BLOCK] < HEAD_DIM) if head == 0 else (lane[:BLOCK] >= HEAD_DIM)
            at = 2 * rows_at + (2 * part + head) * BLOCK
            masked_to[pair, pl.ds(at, BLOCK), :PAIR] = jnp.where(keep, piece, zero[:BLOCK])


def attend_kernel(groups, first, *refs):
    refs = list(refs)
    lab_s, lab_c, x_ref = refs[:3]
    refs = refs[3:]
    if first:
        gain, shift = refs[:2]
        refs = refs[2:]
    weights, biases = refs[:groups], refs[groups : 2 * groups]
    refs = refs[2 * groups :]
    if first:
        normed_ref, normed_t = refs[:2]
        refs = refs[2:]
    qkv = refs[:groups]
    mixed_ref, mixed_t, lse_ref, qm, ke, vt = refs[groups:]
    length = x_ref.shape[0]
    blocks = length // BLOCK

    def prepare(tile, carry):
        at = pl.multiple_of(tile * ROWS, ROWS)
        rows = pl.ds(at, ROWS)
        if first:
            xhat, _ = centred(x_ref[rows, :].astype(F32))
            x = (xhat * gain[...] + shift[...]).astype(BF16)
            normed_ref[rows, :] = x
            normed_t[:, rows] = x.T
        else:
            x = x_ref[rows, :]
        same = lane_of((ROWS, BLOCK)) == lab_c[rows, :]
        hot = jnp.where(same, 1.0, 0.0).astype(BF16)
        cold = jnp.where(same, 0.0, MASKED).astype(BF16)
        for g in range(groups):
            y = dot(x, weights[g][...]) + biases[g][...]
            q = (y[:, :PAIR] * HEAD_DIM ** (-0.5)).astype(BF16)
            k = y[:, PAIR : 2 * PAIR].astype(BF16)
            v = y[:, 2 * PAIR :].astype(BF16)
            qkv[g][rows, :PAIR] = q
            qkv[g][rows, PAIR : 2 * PAIR] = k
            qkv[g][rows, 2 * PAIR :] = v
            fill_heads(at, q, qm, g)
            for part in range(ROWS // BLOCK):
                for head in range(2):
                    to = pl.ds(2 * at + (2 * part + head) * BLOCK, BLOCK)
                    qm[g, to, PAIR:] = hot[part * BLOCK : (part + 1) * BLOCK]
            ke[g, rows, :PAIR] = k
            ke[g, rows, PAIR:] = cold
            vt[g, :, rows] = v.T
        return carry

    lax.fori_loop(0, length // ROWS, prepare, 0)

    def body(at, base, span):
        keys = pl.ds(pl.multiple_of(base * BLOCK, BLOCK), span * BLOCK)
        rows = pl.ds(pl.multiple_of(at * BLOCK, BLOCK), BLOCK)
        both = pl.ds(pl.multiple_of(at * 2 * BLOCK, 2 * BLOCK), 2 * BLOCK)
        for g in range(groups):
            scores = dot(ke[g, keys, :], qm[g, both, :], NT)
            peak = jnp.max(scores, axis=0, keepdims=True)
            raised = jnp.exp(scores - peak)
            total = jnp.sum(raised, axis=0, keepdims=True)
            out = dot(vt[g, :, keys], raised.astype(BF16)) * (1.0 / total)
            out = jnp.concatenate([out[:HEAD_DIM, :BLOCK], out[HEAD_DIM:, BLOCK:]], axis=0)
            mixed_t[g * PAIR : (g + 1) * PAIR, rows] = out.astype(BF16)
            mixed_ref[rows, g * PAIR : (g + 1) * PAIR] = out.T.astype(BF16)
            lse = peak + jnp.log(total)
            lse_ref[2 * g : 2 * g + 1, rows] = lse[:, :BLOCK]
            lse_ref[2 * g + 1 : 2 * g + 2, rows] = lse[:, BLOCK:]

    each_query_block(lab_s, blocks, body)


def attend(lab_s, lab_c, x, norm, weights, biases):
    groups = len(weights)
    length, width = x.shape
    first = norm is not None
    outs = [shape((length, width), BF16), shape((width, length), BF16)] if first else []
    outs += [shape((length, 3 * PAIR), BF16)] * groups
    outs += [
        shape((length, groups * PAIR), BF16),
        shape((groups * PAIR, length), BF16),
        shape((2 * groups, length), F32),
    ]
    args = [lab_s, lab_c, x] + (list(norm) if first else []) + list(weights) + list(biases)
    scratch = [
        pltpu.VMEM((groups, 2 * length, 2 * PAIR), BF16),
        pltpu.VMEM((groups, length, 2 * PAIR), BF16),
        pltpu.VMEM((groups, PAIR, length), BF16),
    ]
    flops = groups * (2 * length * width * 3 * PAIR + 8 * length * length * PAIR)
    got = call(
        functools.partial(attend_kernel, groups, first),
        outs,
        [SMEM] + [VMEM] * (len(args) - 1),
        scratch,
        flops,
        *args,
    )
    head = got[:2] if first else []
    got = got[len(head) :]
    return head, got[:groups], got[groups], got[groups + 1], got[groups + 2]


def join_kernel(parts, frames, bias, gain, shift, *refs):
    mixed, weights = refs[:parts], refs[parts : 2 * parts]
    inner_ref, normed_ref, normed_t = refs[2 * parts :]

    def step(tile, carry):
        rows = pl.ds(pl.multiple_of(tile * ROWS, ROWS), ROWS)
        inner = frames[rows, :].astype(F32) + bias[...]
        for m, w in zip(mixed, weights):
            inner += dot(m[rows, :], w[...])
        inner_ref[rows, :] = inner
        xhat, _ = centred(inner)
        normed = (xhat * gain[...] + shift[...]).astype(BF16)
        normed_ref[rows, :] = normed
        normed_t[:, rows] = normed.T
        return carry

    lax.fori_loop(0, frames.shape[0] // ROWS, step, 0)


def join(frames, bias, gain, shift, mixed, weights):
    length, width = frames.shape
    args = [frames, bias, gain, shift] + list(mixed) + list(weights)
    return call(
        functools.partial(join_kernel, len(mixed)),
        [shape((length, width), F32), shape((length, width), BF16), shape((width, length), BF16)],
        [VMEM] * len(args),
        [],
        2 * length * width * width,
        *args,
    )


def gelu_both(u):
    falling = jnp.exp(u * u * -0.5)
    t = 1.0 / (1.0 + jnp.abs(u) * (0.3275911 * 0.5**0.5))
    poly = 0.5 * 1.061405429
    for c in (-1.453152027, 1.421413741, -0.284496736, 0.254829592):
        poly = poly * t + 0.5 * c
    tail = poly * t * falling
    phi = jnp.where(u >= 0.0, 1.0 - tail, tail)
    return u * phi, phi + u * falling * (0.5 / jnp.pi) ** 0.5


def feed_kernel(groups, last, *refs):
    refs = list(refs)
    normed, normed_t, cot, cot_t, out_in, two_in = refs[:6]
    ups, up_biases, downs = (refs[6 + i * groups : 6 + (i + 1) * groups] for i in range(3))
    refs = refs[6 + 3 * groups :]
    out_ref, two_ref = refs[:2]
    up_deltas = refs[2 : 2 + groups]
    down_deltas = refs[2 + groups : 2 + 2 * groups]
    bias_deltas = refs[2 + 2 * groups : 2 + 3 * groups]
    act_s, delta_s = refs[2 + 3 * groups :]
    length = normed.shape[0]
    for g in range(groups):
        bias_deltas[g][...] = jnp.zeros_like(bias_deltas[g])

        def step(tile, carry):
            rows = pl.ds(pl.multiple_of(tile * ROWS, ROWS), ROWS)
            u = dot(normed[rows, :], ups[g][...]) + up_biases[g][...]
            back = dot(cot[rows, :], downs[g][...], NT)
            act, slope = gelu_both(u)
            act = act.astype(BF16)
            delta = (back * slope).astype(BF16)
            act_s[rows, :] = act
            delta_s[rows, :] = delta
            source_out, source_two = (out_in, two_in) if g == 0 else (out_ref, two_ref)
            out_ref[rows, :] = source_out[rows, :] + dot(act, downs[g][...])
            fresh = dot(delta, ups[g][...], NT)
            if g == 0 and two_in is out_in:
                two_ref[rows, :] = fresh
            else:
                two_ref[rows, :] = source_two[rows, :] + fresh
            bias_deltas[g][...] += jnp.sum(delta.astype(F32), axis=0, keepdims=True)
            return carry

        lax.fori_loop(0, length // ROWS, step, 0)
        up_deltas[g][...] = dot(normed_t[...], delta_s[...]).astype(BF16)
        down_deltas[g][...] = dot(cot_t[...], act_s[...]).T.astype(BF16)


def feed(normed, normed_t, cot, cot_t, out_sum, two_sum, ups, up_biases, downs):
    groups = len(ups)
    length, width = normed.shape
    hidden = ups[0].shape[1]
    args = [normed, normed_t, cot, cot_t, out_sum, two_sum] + list(ups) + list(up_biases) + list(downs)
    outs = [shape((length, width), F32)] * 2
    outs += [shape((width, hidden), BF16)] * groups
    outs += [shape((hidden, width), BF16)] * groups
    outs += [shape((1, hidden), F32)] * groups
    got = call(
        functools.partial(feed_kernel, groups, False),
        outs,
        [VMEM] * len(args),
        [pltpu.VMEM((length, hidden), BF16)] * 2,
        12 * groups * length * width * hidden,
        *args,
    )
    return (
        got[0],
        got[1],
        got[2 : 2 + groups],
        got[2 + groups : 2 + 2 * groups],
        got[2 + 2 * groups :],
    )


def turn_kernel(parts, inner_ref, out_ref, down_bias, two_ref, cot, gain, *refs):
    mixed, mixed_t, weights = (refs[i * parts : (i + 1) * parts] for i in range(3))
    refs = refs[3 * parts :]
    layer_ref, delta_ref, sums_ref, inner_rows = refs[:4]
    branch_s = refs[-1]
    out_deltas, delta_mixed = refs[4 : 4 + parts], refs[4 + parts : 4 + 2 * parts]
    length, width = inner_ref.shape
    sums_ref[...] = jnp.zeros_like(sums_ref)
    features = sum(m.shape[1] for m in mixed)
    heads = features // HEAD_DIM

    def step(tile, carry):
        rows = pl.ds(pl.multiple_of(tile * ROWS, ROWS), ROWS)
        inner = inner_ref[rows, :]
        layer_ref[rows, :] = (inner + out_ref[rows, :] + down_bias[...]).astype(BF16)
        xhat, scale = centred(inner)
        two = two_ref[rows, :]
        dy = cot[rows, :].astype(F32)
        e = two * gain[...]
        lean = jnp.mean(e, axis=-1, keepdims=True)
        pull = jnp.mean(e * xhat, axis=-1, keepdims=True)
        delta = dy + scale * (e - lean - xhat * pull)
        delta_ref[rows, :] = delta
        branch = delta.astype(BF16)
        branch_s[rows, :] = branch
        sums_ref[0:1, :] += jnp.sum(two * xhat, axis=0, keepdims=True)
        sums_ref[1:2, :] += jnp.sum(two, axis=0, keepdims=True)
        sums_ref[2:3, :] += jnp.sum(branch.astype(F32), axis=0, keepdims=True)
        sums_ref[3:4, :] += jnp.sum(dy, axis=0, keepdims=True)
        head_at = 0
        for m, w, dm in zip(mixed, weights, delta_mixed):
            back = dot(branch, w[...], NT).astype(BF16)
            dm[rows, :] = back
            product = back.astype(F32) * m[rows, :].astype(F32)
            high = product.astype(BF16)
            low = (product - high.astype(F32)).astype(BF16)
            here = m.shape[1] // HEAD_DIM
            dims = (2 * here, m.shape[1])
            picks = lax.broadcasted_iota(jnp.int32, dims, 0) == lane_of(dims) // HEAD_DIM
            ones = jnp.where(picks, 1.0, 0.0).astype(BF16)
            sums = dot(ones, high, NT) + dot(ones, low, NT)
            inner_rows[head_at : head_at + here, rows] = sums[:here]
            head_at += here
        return carry

    lax.fori_loop(0, length // ROWS, step, 0)
    for mt, od in zip(mixed_t, out_deltas):
        od[...] = dot(mt[...], branch_s[...]).astype(BF16)


def turn(inner, out_sum, down_bias, two_sum, cot, gain, mixed, mixed_t, weights):
    length, width = inner.shape
    parts = len(mixed)
    args = [inner, out_sum, down_bias, two_sum, cot, gain]
    args += list(mixed) + list(mixed_t) + list(weights)
    features = sum(m.shape[1] for m in mixed)
    outs = [
        shape((length, width), BF16),
        shape((length, width), F32),
        shape((8, width), F32),
        shape((features // HEAD_DIM, length), F32),
    ]
    outs += [shape(w.shape, BF16) for w in weights]
    outs += [shape(m.shape, BF16) for m in mixed]
    got = call(
        functools.partial(turn_kernel, parts),
        outs,
        [VMEM] * len(args),
        [pltpu.VMEM((length, width), BF16)],
        4 * length * width * width,
        *args,
    )
    return got[0], got[1], got[2], got[3], got[4 : 4 + parts], got[4 + parts :]


def attend_back_kernel(groups, dm_at, lab_s, lab_c, normed_t, lse_ref, inner_ref, *refs):
    qkv, dms = refs[:groups], refs[groups : 2 * groups]
    refs = refs[2 * groups :]
    deltas, changes, sums = (refs[i * groups : (i + 1) * groups] for i in range(3))
    qm, ke, ve, dmm, kt, dk, dv = refs[3 * groups :]
    length = normed_t.shape[1]
    blocks = length // BLOCK

    def prepare(tile, carry):
        at = pl.multiple_of(tile * ROWS, ROWS)
        rows = pl.ds(at, ROWS)
        same = lane_of((ROWS, BLOCK)) == lab_c[rows, :]
        hot = jnp.where(same, 1.0, 0.0).astype(BF16)
        cold = jnp.where(same, 0.0, MASKED).astype(BF16)
        for g in range(groups):
            q = qkv[g][rows, :PAIR]
            k = qkv[g][rows, PAIR : 2 * PAIR]
            fill_heads(at, q, qm, g)
            for part in range(ROWS // BLOCK):
                for head in range(2):
                    to = pl.ds(2 * at + (2 * part + head) * BLOCK, BLOCK)
                    qm[g, to, PAIR:] = hot[part * BLOCK : (part + 1) * BLOCK]
            fill_heads(at, dms[g][rows, :], dmm, g)
            ke[g, rows, :PAIR] = k
            ke[g, rows, PAIR:] = cold
            ve[g, rows, :] = qkv[g][rows, 2 * PAIR :]
            kt[g, :, rows] = k.T
            dk[g, rows, :] = jnp.zeros((ROWS, PAIR), F32)
            dv[g, rows, :] = jnp.zeros((ROWS, PAIR), F32)
        return carry

    lax.fori_loop(0, length // ROWS, prepare, 0)

    def body(at, base, span):
        rows = pl.ds(pl.multiple_of(at * BLOCK, BLOCK), BLOCK)
        both = pl.ds(pl.multiple_of(at * 2 * BLOCK, 2 * BLOCK), 2 * BLOCK)
        for g in range(groups):
            queries = qm[g, both, :]
            downs = dmm[g, both, :]
            lse = jnp.concatenate([lse_ref[2 * g : 2 * g + 1, rows], lse_ref[2 * g + 1 : 2 * g + 2, rows]], axis=1)
            pull = jnp.concatenate([inner_ref[2 * g : 2 * g + 1, rows], inner_ref[2 * g + 1 : 2 * g + 2, rows]], axis=1)
            dqt = jnp.zeros((PAIR, 2 * BLOCK), F32)
            done = 0
            while done < span:
                size = min(2, span - done)
                keys = pl.ds(pl.multiple_of((base + done) * BLOCK, BLOCK), size * BLOCK)
                scores = dot(ke[g, keys, :], queries, NT)
                probs = jnp.exp(scores - lse)
                slope = dot(ve[g, keys, :], downs, NT)
                delta = (probs * (slope - pull)).astype(BF16)
                dv[g, keys, :] += dot(probs.astype(BF16), downs)
                dk[g, keys, :] += dot(delta, queries[:, :PAIR])
                dqt += dot(kt[g, :, keys], delta)
                done += size
            dqt = jnp.concatenate([dqt[:HEAD_DIM, :BLOCK], dqt[HEAD_DIM:, BLOCK:]], axis=0)
            dq = dqt.T.astype(BF16).astype(F32) * HEAD_DIM ** (-0.5)
            deltas[g][rows, :PAIR] = dq.astype(BF16)

    each_query_block(lab_s, blocks, body)
    for g in range(groups):
        deltas[g][:, PAIR : 2 * PAIR] = dk[g].astype(BF16)
        deltas[g][:, 2 * PAIR :] = dv[g].astype(BF16)
        changes[g][...] = dot(normed_t[...], deltas[g][...]).astype(BF16)
        sums[g][...] = jnp.sum(deltas[g][...].astype(F32), axis=0, keepdims=True)


def attend_back(lab_s, lab_c, normed_t, lse, inner, qkv, dms):
    groups = len(qkv)
    width, length = normed_t.shape
    args = [lab_s, lab_c, normed_t, lse, inner] + list(qkv) + list(dms)
    outs = [shape((length, 3 * PAIR), BF16)] * groups
    outs += [shape((width, 3 * PAIR), BF16)] * groups
    outs += [shape((1, 3 * PAIR), F32)] * groups
    scratch = [
        pltpu.VMEM((groups, 2 * length, 2 * PAIR), BF16),
        pltpu.VMEM((groups, length, 2 * PAIR), BF16),
        pltpu.VMEM((groups, length, PAIR), BF16),
        pltpu.VMEM((groups, 2 * length, PAIR), BF16),
        pltpu.VMEM((groups, PAIR, length), BF16),
        pltpu.VMEM((groups, length, PAIR), F32),
        pltpu.VMEM((groups, length, PAIR), F32),
    ]
    got = call(
        functools.partial(attend_back_kernel, groups, 0),
        outs,
        [SMEM] + [VMEM] * (len(args) - 1),
        scratch,
        groups * (2 * length * width * 3 * PAIR + 20 * length * length * PAIR),
        *args,
    )
    return got[:groups], got[groups : 2 * groups], got[2 * groups :]


def close_kernel(groups, frames, delta_ref, gain, *refs):
    deltas, weights = refs[:groups], refs[groups : 2 * groups]
    out_ref, sums_ref = refs[2 * groups :]
    sums_ref[...] = jnp.zeros_like(sums_ref)

    def step(tile, carry):
        rows = pl.ds(pl.multiple_of(tile * ROWS, ROWS), ROWS)
        one = jnp.zeros((ROWS, frames.shape[1]), F32)
        for d, w in zip(deltas, weights):
            one += dot(d[rows, :], w[...], NT)
        xhat, scale = centred(frames[rows, :].astype(F32))
        e = one * gain[...]
        lean = jnp.mean(e, axis=-1, keepdims=True)
        pull = jnp.mean(e * xhat, axis=-1, keepdims=True)
        out_ref[rows, :] = (delta_ref[rows, :] + scale * (e - lean - xhat * pull)).astype(BF16)
        sums_ref[0:1, :] += jnp.sum(one * xhat, axis=0, keepdims=True)
        sums_ref[1:2, :] += jnp.sum(one, axis=0, keepdims=True)
        return carry

    lax.fori_loop(0, frames.shape[0] // ROWS, step, 0)


def close(frames, delta, gain, deltas, weights):
    length, width = frames.shape
    args = [frames, delta, gain] + list(deltas) + list(weights)
    return call(
        functools.partial(close_kernel, len(deltas)),
        [shape((length, width), BF16), shape((8, width), F32)],
        [VMEM] * len(args),
        [],
        6 * length * width * width,
        *args,
    )


PLANE = ("aa", "ba")


def plane_swap(value, step, size):
    return lax.ppermute(value, PLANE, [(i, i ^ step) for i in range(size)])


def dp_swap(value, step, size):
    return lax.ppermute(value, "dp", [(i, i ^ step) for i in range(size)])


def halves(value, axis, core):
    low, high = jnp.split(value, 2, axis=axis)
    return jnp.where(core == 0, low, high), jnp.where(core == 0, high, low)


def unhalve(mine, other, axis, core):
    low = jnp.where(core == 0, mine, other)
    high = jnp.where(core == 0, other, mine)
    return jnp.concatenate([low, high], axis=axis)


def shards(
    frames,
    segment_ids,
    cotangent,
    first_gain,
    first_shift,
    query_weight,
    query_bias,
    key_weight,
    value_weight,
    value_bias,
    out_weight,
    out_bias,
    second_gain,
    second_shift,
    up_weight,
    up_bias,
    down_weight,
    down_bias,
):
    length, width = frames.shape[1:]
    planes = lax.axis_size(PLANE)
    dp_size = lax.axis_size("dp")
    core = lax.axis_index("dp") % 2
    head_cols = query_weight.shape[1]
    groups = width // PAIR
    per_group = planes // groups

    def row(v):
        return v.astype(F32)[None, :]

    qkv_half = [halves(w, 1, core) for w in (query_weight, key_weight, value_weight)]
    half_cols = head_cols // 2
    zero_bias = jnp.zeros_like(query_bias)
    bias_half = [halves(b, 0, core) for b in (query_bias, zero_bias, value_bias)]
    qkv_own = [
        jnp.concatenate(
            [jnp.concatenate([w[h] for w in qkv_half], axis=1), jnp.concatenate([b[h] for b in bias_half])[None, :]],
            axis=0,
        )
        for h in range(2)
    ]
    out_own = halves(out_weight, 0, core)
    up_own = halves(up_weight, 1, core)
    up_bias_own = halves(up_bias, 0, core)
    down_own = halves(down_weight, 0, core)

    def gathered(own):
        pieces = [own]
        for r in range(1, planes):
            near = plane_swap(own[0], r, planes)
            pieces.append((near, dp_swap(near, 1, dp_size)))
        return pieces

    qkv_pieces = gathered(qkv_own)
    out_pieces = gathered(out_own)
    up_pieces = gathered(up_own)
    up_bias_pieces = gathered(up_bias_own)
    down_pieces = gathered(down_own)

    def group_pieces(pieces, g):
        return [p for r in range(g * per_group, (g + 1) * per_group) for p in pieces[r]]

    qkv_w, qkv_b, out_w, up_w, up_b, down_w = [], [], [], [], [], []
    for g in range(groups):
        parts = group_pieces(qkv_pieces, g)
        joined = jnp.concatenate(
            [p[:, i * half_cols : (i + 1) * half_cols] for i in range(3) for p in parts], axis=1
        )
        qkv_w.append(joined[:width])
        qkv_b.append(joined[width:].astype(F32))
        out_w.append(jnp.concatenate(group_pieces(out_pieces, g), axis=0))
        up_w.append(jnp.concatenate(group_pieces(up_pieces, g), axis=1))
        up_b.append(row(jnp.concatenate(group_pieces(up_bias_pieces, g), axis=0)))
        down_w.append(jnp.concatenate(group_pieces(down_pieces, g), axis=0))

    x = frames[0]
    dy = cotangent[0]
    lab_c = segment_ids.reshape(length, 1)
    gain_one, shift_one, gain_two, shift_two = map(row, (first_gain, first_shift, second_gain, second_shift))

    (normed, normed_t), qkv0, mixed0, mixed_t0, lse0 = attend(
        segment_ids, lab_c, x, (gain_one, shift_one), qkv_w[:1], qkv_b[:1]
    )
    _, qkv1, mixed1, mixed_t1, lse1 = attend(segment_ids, lab_c, normed, None, qkv_w[1:], qkv_b[1:])
    qkv = list(qkv0) + list(qkv1)
    out_w_parts = [out_w[0], jnp.concatenate(out_w[1:], axis=0)]
    inner, normed_two, normed_two_t = join(x, row(out_bias), gain_two, shift_two, [mixed0, mixed1], out_w_parts)
    dy_t = dy.T
    zero = jnp.zeros((length, width), F32)
    out_sum, two_sum, up_d, down_d, upb_d = feed(
        normed_two, normed_two_t, dy, dy_t, zero, zero, up_w, up_b, down_w
    )
    layer, delta, sums, inner_rows, out_d, dms = turn(
        inner, out_sum, row(down_bias), two_sum, dy, gain_two, [mixed0, mixed1], [mixed_t0, mixed_t1], out_w_parts
    )
    out_delta = jnp.concatenate(out_d, axis=0)
    dm_groups = [dms[0]] + [dms[1][:, i * PAIR : (i + 1) * PAIR] for i in range(groups - 1)]
    lse = jnp.concatenate([lse0, lse1], axis=0)
    deltas, changes, change_sums = [], [], []
    for g in list(range(1, groups)) + [0]:
        d, c, s = attend_back(
            segment_ids, lab_c, normed_t, lse[2 * g : 2 * g + 2], inner_rows[2 * g : 2 * g + 2], [qkv[g]], [dm_groups[g]]
        )
        deltas.append(d[0])
        changes.append(c[0])
        change_sums.append(s[0])
    order = list(range(1, groups)) + [0]
    frames_delta, close_sums = close(x, delta, gain_one, deltas, [qkv_w[g] for g in order])
    by_group = {g: i for i, g in enumerate(order)}

    def reduced(value, axis):
        size = value.shape[axis] // (2 * planes)

        def piece(at):
            return lax.slice_in_dim(value, at * size, (at + 1) * size, axis=axis)

        mine = []
        for r in range(planes):
            mine.append(piece(2 * r) + dp_swap(piece(2 * r + 1), 1, dp_size))
        total = mine[0].astype(F32)
        for r in range(1, planes):
            total += plane_swap(mine[r], r, planes).astype(F32)
        total = total.astype(BF16)
        wide = total.astype(F32)
        for k in range(2, dp_size, 2):
            wide += dp_swap(total, k, dp_size).astype(F32)
        wide = wide.astype(BF16)
        return unhalve(wide, dp_swap(wide, 1, dp_size), axis, core).astype(F32)

    def joint(i):
        return jnp.concatenate([changes[by_group[g]][:, i * PAIR : (i + 1) * PAIR] for g in range(groups)], axis=1)

    def joint_sum(i):
        return jnp.concatenate([change_sums[by_group[g]][0, i * PAIR : (i + 1) * PAIR] for g in range(groups)], axis=0)

    query_change = reduced(joint(0), 1)
    key_change = reduced(joint(1), 1)
    value_change = reduced(joint(2), 1)
    qbias_change = reduced(joint_sum(0), 0)
    vbias_change = reduced(joint_sum(2), 0)
    out_change = reduced(out_delta, 0)
    up_change = reduced(jnp.concatenate(up_d, axis=1), 1)
    down_change = reduced(jnp.concatenate(down_d, axis=0), 0)
    upbias_change = reduced(jnp.concatenate(upb_d, axis=1)[0], 0)

    small = jnp.concatenate([close_sums[:2], sums[:4]], axis=0)
    small = small + dp_swap(small, 1, dp_size)
    total = small
    for r in range(1, planes):
        total += plane_swap(small, r, planes)
    small = total
    for k in range(2, dp_size, 2):
        total += dp_swap(small, k, dp_size)
    return (
        layer[None],
        frames_delta[None],
        total[0],
        total[1],
        query_change,
        qbias_change,
        key_change,
        value_change,
        vbias_change,
        out_change,
        total[4],
        total[2],
        total[3],
        up_change,
        upbias_change,
        down_change,
        total[5],
    )


def solution(mesh):
    rows = P(("dp", "aa", "ba"), None, None)
    cols = P(None, ("aa", "ba"))
    flat = P(("aa", "ba"))
    down = P(("aa", "ba"), None)
    placed = (
        rows, P(("dp", "aa", "ba"), None), rows, P(), P(), cols, flat, cols, cols, flat,
        down, P(), P(), P(), cols, flat, down, P(),
    )
    outs = (
        rows, rows, P(), P(), cols, flat, cols, cols, flat, down, P(), P(), P(), cols, flat, down, P(),
    )
    return jax.shard_map(shards, mesh=mesh, in_specs=placed, out_specs=outs, check_vma=False)
```

time: 828 us -> 440 us (0.53)
  waiting for transfers between devices: 400 us -> 106 us
  matrix products: 157 us -> 0 us
  starting transfers between devices: 1.42 us -> 130 us
  Pallas kernels: 0 us -> 121 us
  blocking collectives: 99.6 us -> 0 us
  local copies, waits for them, and re-layouts: 72.1 us -> 37.4 us
  other arithmetic: 70.3 us -> 36.2 us
  between operations: 15.8 us -> 2.09 us
    dot_general x68 -> x0, matrix products: 157 us -> none  [the longest x28 65.7 us: project_back(): lax.dot_general(left, right, (((1,), (1,)), ((), ())), preferred_element_...]
    unnamed x18 -> x0, waiting for transfers between devices: 141 us -> none
    all_gather x4 -> x0, waiting for transfers between devices: 132 us -> none  [the longest x1 52.2 us: shards(): feed_normed = lax.all_gather(normed_two, ('aa', 'ba'), axis=0, tiled=True)]
    ppermute x0 -> x136, starting transfers between devices: none -> 130 us  [the longest x91 73.2 us: dp_swap(): return lax.ppermute(value, 'dp', [(i, i ^ step) for i in range(size)])]
    pallas_call x0 -> x10, Pallas kernels: none -> 121 us  [call(): pl.pallas_call(body, out_shape=out_shape, in_specs=in_specs, out_specs=[V...]
    ppermute x0 -> x136, waiting for transfers between devices: none -> 106 us  [the longest x91 65.9 us: dp_swap(): return lax.ppermute(value, 'dp', [(i, i ^ step) for i in range(size)])]
    reduce_scatter x3 -> x0, waiting for transfers between devices: 91 us -> none  [the longest x1 55.1 us: shards(): lax.psum_scatter(project(window_rows(mixed_rows, row_count), out_here).re...]
    psum x2 -> x0, blocking collectives: 55.5 us -> none  [the longest x1 39.5 us: shards(): lax.psum((gain_one_change, shift_one_change, gain_two_change, shift_two_c...]
  transfers between devices with their start and end apart: 13 -> 136, of which waited for: 11 -> 59; matrix products, arithmetic and copies ran while one was open for 9% -> 16% of each run, Pallas kernels for 0% -> 19%
where the time goes in v1:
time: 440 us; the launch traced here: 433 us
  starting transfers between devices  130 us (30%)
  Pallas kernels  121 us (28%)
  waiting for transfers between devices  106 us (24%)
  local copies, waits for them, and re-layouts  37.4 us (8%)
  other arithmetic  36.2 us (8%)
    pallas_call x10, Pallas kernels, call(): pl.pallas_call(body, out_shape=out_shape, in_specs=in_specs, out_specs=[V...  121 us
    ppermute x91, starting transfers between devices, dp_swap(): return lax.ppermute(value, 'dp', [(i, i ^ step) for i in range(size)])  73.2 us
    ppermute x91, waiting for transfers between devices, dp_swap(): return lax.ppermute(value, 'dp', [(i, i ^ step) for i in range(size)])  65.9 us
    ppermute x45, starting transfers between devices, plane_swap(): return lax.ppermute(value, PLANE, [(i, i ^ step) for i in range(size)])  56.8 us
    ppermute x45, waiting for transfers between devices, plane_swap(): return lax.ppermute(value, PLANE, [(i, i ^ step) for i in range(size)])  39.7 us
    slice x20, local copies, waits for them, and re-layouts, piece(): return lax.slice_in_dim(value, at * size, (at + 1) * size, axis=axis)  14.1 us
  transfers between devices with their start and end apart: 136, of which 59 were waited for; matrix products, arithmetic and copies ran while one was open for 16% of the time, Pallas kernels for 19%

profile of v1, /device:TPU:0, one launch (start us, length us, event | category | flops | bytes accessed | tf_op | source)
XLA Modules:
  0.0 432.8 jit_solution(4274055149597994511)
XLA Ops:
  1.4 3.9 collective-permute-start.22
  6.8 2.9 collective-permute-start.10
  24.0 11.2 %shard_map.305 = (bf16[1024,512]{1,0:T(8,128)(2,1)}, bf16[512,1024]{1,0:T(8,128)(2,1)}, bf16[1024,384]{1,0:T(8,128)(2,1)}, bf16[1024,128]{1,0:T(8,128)(2,1)}, bf...) custom-call(s32[1,1024]{1,0:T(1,128)} %lab_s.7, s32[1024,1]{1,0:T(8,128)} %copy.36.refs_1_.lab_c, bf16[1024,512]{1,0:T(8,128)(2,1)} %bitcast.78, ...), custom_call_target="tpu_custom_call" | custom-call | flops 1476395008 | bytes 4871680 | tf_op jit(solution)/shard_map/pallas_call | solution.py:35
  51.5 7.4 %collective-permute-done.2 = bf16[513,192]{1,0:T(8,128)(2,1)S(1)} collective-permute-done((bf16[513,192]{1,0:T(8,128)(2,1)S(1)}, bf16[513,192]{1,0:T(8,128)(2,1)S(1)}, u32[]{:S(2)}, u32[]{:S(2)}) %collective-permute-start.2) | collective-permute-done | bytes 197024 | tf_op jit(solution)/shard_map/ppermute | solution.py:518
  76.1 16.5 %shard_map.306 = (bf16[1024,384]{1,0:T(8,128)(2,1)}, bf16[1024,384]{1,0:T(8,128)(2,1)}, bf16[1024,384]{1,0:T(8,128)(2,1)}, bf16[1024,384]{1,0:T(8,128)(2,1)}, bf...) custom-call(s32[1,1024]{1,0:T(1,128)} %lab_s.7, s32[1024,1]{1,0:T(8,128)} %copy.36.refs_1_.lab_c, ...), custom_call_target="tpu_custom_call" | custom-call | flops 4429185024 | bytes 6197760 | tf_op jit(solution)/shard_map/pallas_call | solution.py:35
  92.6 3.4 collective-permute-start.24
  98.1 5.9 %shard_map.307 = (f32[1024,512]{1,0:T(8,128)}, bf16[1024,512]{1,0:T(8,128)(2,1)}, bf16[512,1024]{1,0:T(8,128)(2,1)}) custom-call(bf16[1024,512]{1,0:T(8,128)(2,1)} %bitcast.79, f32[1,512]{1,0:T(1,128)} %bitcast.86, f32[1,512]{1,0:T(1,128)} %bitcast.81, f32[1,512]{1,0:T(1,128)} %bitcast.87, bf16[1024,128]{1,0:T(8,128)(2,1)} %get-tuple-element.68.refs_0_, ...), custom_call_target="tpu_custom_call" | custom-call | flops 536870912 | bytes 6821888 | tf_op jit(solution)/shard_map/pallas_call | solution.py:35
  115.5 29.3 %shard_map.308 = (f32[1024,512]{1,0:T(8,128)}, f32[1024,512]{1,0:T(8,128)}, bf16[512,512]{1,0:T(8,128)(2,1)}, bf16[512,512]{1,0:T(8,128)(2,1)}, bf16[512,512]{1,...) custom-call(bf16[1024,512]{1,0:T(8,128)(2,1)} %get-tuple-element.72., ...), custom_call_target="tpu_custom_call" | custom-call | flops 12884901888 | bytes 20987904 | tf_op jit(solution)/shard_map/pallas_call | solution.py:35
  144.8 10.3 %shard_map.309 = (bf16[1024,512]{1,0:T(8,128)(2,1)}, f32[1024,512]{1,0:T(8,128)}, f32[8,512]{1,0:T(8,128)}, f32[8,1024]{1,0:T(8,128)}, bf16[128,512]{1,0:T(8,128...) custom-call(f32[1024,512]{1,0:T(8,128)} %get-tuple-element.71.inner_ref, ...), custom_call_target="tpu_custom_call" | custom-call | flops 1073741824 | bytes 14733312 | tf_op jit(solution)/shard_map/pallas_call | solution.py:35
  160.9 10.1 %shard_map.313 = (bf16[1024,384]{1,0:T(8,128)(2,1)}, bf16[512,384]{1,0:T(8,128)(2,1)}, f32[1,384]{1,0:T(1,128)}) custom-call(s32[1,1024]{1,0:T(1,128)} %lab_s.7, s32[1024,1]{1,0:T(8,128)} %copy.36.refs_1_.lab_c, bf16[512,1024]{1,0:T(8,128)(2,1)} %get-tuple-element.80.normed_t, f32[2,1024]{1,0:T(2,128)} %get-tuple-element.90.lse_ref, ...), custom_call_target="tpu_custom_call" | custom-call | flops 3087007744 | bytes 3302912 | tf_op jit(solution)/shard_map/pallas_call | solution.py:35
  181.2 10.2 %shard_map.312 = (bf16[1024,384]{1,0:T(8,128)(2,1)}, bf16[512,384]{1,0:T(8,128)(2,1)}, f32[1,384]{1,0:T(1,128)}) custom-call(s32[1,1024]{1,0:T(1,128)} %lab_s.7, s32[1024,1]{1,0:T(8,128)} %copy.36.refs_1_.lab_c, bf16[512,1024]{1,0:T(8,128)(2,1)} %get-tuple-element.80.normed_t, f32[2,1024]{1,0:T(2,128)} %get-tuple-element.200.lse_ref, ...), custom_call_target="tpu_custom_call" | custom-call | flops 3087007744 | bytes 3302912 | tf_op jit(solution)/shard_map/pallas_call | solution.py:35
  193.6 10.0 %shard_map.311 = (bf16[1024,384]{1,0:T(8,128)(2,1)}, bf16[512,384]{1,0:T(8,128)(2,1)}, f32[1,384]{1,0:T(1,128)}) custom-call(s32[1,1024]{1,0:T(1,128)} %lab_s.7, s32[1024,1]{1,0:T(8,128)} %copy.36.refs_1_.lab_c, bf16[512,1024]{1,0:T(8,128)(2,1)} %get-tuple-element.80.normed_t, f32[2,1024]{1,0:T(2,128)} %get-tuple-element.201.lse_ref, ...), custom_call_target="tpu_custom_call" | custom-call | flops 3087007744 | bytes 3302912 | tf_op jit(solution)/shard_map/pallas_call | solution.py:35
  204.9 10.0 %shard_map.310 = (bf16[1024,384]{1,0:T(8,128)(2,1)}, bf16[512,384]{1,0:T(8,128)(2,1)}, f32[1,384]{1,0:T(1,128)}) custom-call(s32[1,1024]{1,0:T(1,128)} %lab_s.7, s32[1024,1]{1,0:T(8,128)} %copy.36.refs_1_.lab_c, bf16[512,1024]{1,0:T(8,128)(2,1)} %get-tuple-element.80.normed_t, f32[2,1024]{1,0:T(2,128)} %get-tuple-element.202.lse_ref, ...), custom_call_target="tpu_custom_call" | custom-call | flops 3087007744 | bytes 3302912 | tf_op jit(solution)/shard_map/pallas_call | solution.py:35
  214.9 8.1 %shard_map.314 = (bf16[1024,512]{1,0:T(8,128)(2,1)}, f32[8,512]{1,0:T(8,128)}) custom-call(bf16[1024,512]{1,0:T(8,128)(2,1)} %bitcast.80, f32[1024,512]{1,0:T(8,128)} %get-tuple-element.79.delta_ref, f32[1,512]{1,0:T(1,128)} %bitcast.84, bf16[1024,384]{1,0:T(8,128)(2,1)} %get-tuple-element.85.refs_0_, bf16[1024,384]{1,0:T(8,128)(2,1)} %get-tuple-element.87.refs_1_, ...), custom_call_target="tpu_custom_call" | custom-call | flops 1610612736 | bytes 8931328 | tf_op jit(solution)/shard_map/pallas_call | solution.py:35
  224.2 2.4 collective-permute-start.82
  229.4 2.7 collective-permute-start.54
  240.4 3.9 collective-permute-start.90
  246.4 2.5 collective-permute-done.89
  251.7 2.5 collective-permute-done.57
  254.2 3.5 collective-permute-done.55
  266.3 2.9 collective-permute-start.121
  321.1 3.8 collective-permute-done.79
  327.0 8.1 %collective-permute-done.78 = bf16[512,64]{1,0:T(8,128)(2,1)S(1)} collective-permute-done((bf16[512,64]{1,0:T(8,128)(2,1)S(1)}, bf16[512,64]{1,0:T(8,128)(2,1)S(1)}, u32[]{:S(2)}, u32[]{:S(2)}) %collective-permute-start.78) | collective-permute-done | bytes 65568 | tf_op jit(solution)/shard_map/ppermute | solution.py:522
  339.6 6.5 %collective-permute-done.67 = bf16[512,64]{1,0:T(8,128)(2,1)S(1)} collective-permute-done((bf16[512,64]{1,0:T(8,128)(2,1)S(1)}, bf16[512,64]{1,0:T(8,128)(2,1)S(1)}, u32[]{:S(2)}, u32[]{:S(2)}) %collective-permute-start.67) | collective-permute-done | bytes 65568 | tf_op jit(solution)/shard_map/ppermute | solution.py:522
  350.7 5.3 %collective-permute-done.45 = bf16[512,64]{1,0:T(8,128)(2,1)S(1)} collective-permute-done((bf16[512,64]{1,0:T(8,128)(2,1)S(1)}, bf16[512,64]{1,0:T(8,128)(2,1)S(1)}, u32[]{:S(2)}, u32[]{:S(2)}) %collective-permute-start.45) | collective-permute-done | bytes 65568 | tf_op jit(solution)/shard_map/ppermute | solution.py:522
  358.6 2.7 collective-permute-done.100
  373.0 2.7 collective-permute-done.109
  376.7 5.0 %collective-permute-done.107 = bf16[512,256]{1,0:T(8,128)(2,1)S(1)} collective-permute-done((bf16[512,256]{1,0:T(8,128)(2,1)S(1)}, bf16[512,256]{1,0:T(8,128)(2,1)S(1)}, u32[]{:S(2)}, u32[]{:S(2)}) %collective-permute-start.107) | collective-permute-done | bytes 262176 | tf_op jit(solution)/shard_map/ppermute | solution.py:518
  388.0 4.3 collective-permute-done.129
  395.3 17.6 %collective-permute-start.132 = (bf16[256,512]{1,0:T(8,128)(2,1)S(1)}, bf16[256,512]{1,0:T(8,128)(2,1)S(1)}, u32[]{:S(2)}, u32[]{:S(2)}) collective-permute-start(bf16[256,512]{1,0:T(8,128)(2,1)S(1)} %add_convert_fusion.1), channel_id=1, source_target_pairs={{0,8},{4,12},{8,0},{12,4},{16,24},{20,28},{24,16},{28,20},{1,9},{5... | collective-permute-start | bytes 786440 | tf_op jit(solution)/shard_map/ppermute | solution.py:522
  412.9 6.8 %collective-permute-done.111 = bf16[512,256]{1,0:T(8,128)(2,1)S(1)} collective-permute-done((bf16[512,256]{1,0:T(8,128)(2,1)S(1)}, bf16[512,256]{1,0:T(8,128)(2,1)S(1)}, u32[]{:S(2)}, u32[]{:S(2)}) %collective-permute-start.111) | collective-permute-done | bytes 262176 | tf_op jit(solution)/shard_map/ppermute | solution.py:522
  420.7 8.7 %collective-permute-done.133 = bf16[256,512]{1,0:T(8,128)(2,1)S(1)} collective-permute-done((bf16[256,512]{1,0:T(8,128)(2,1)S(1)}, bf16[256,512]{1,0:T(8,128)(2,1)S(1)}, u32[]{:S(2)}, u32[]{:S(2)}) %collective-permute-start.133) | collective-permute-done | bytes 262176 | tf_op jit(solution)/shard_map/ppermute | solution.py:522
  (492 shorter events, 199.8 us)
Async XLA Ops:
  1.4 36.7 %collective-permute-start.22 = (bf16[256]{0:T(256)(128)(2,1)S(1)}, bf16[256]{0:T(256)(128)(2,1)S(1)}, u32[]{:S(2)}, u32[]{:S(2)}) collective-permute-start(bf16[256]{0:T(256)(128)(2,1)S(1)} %get-tuple-element.239), channel_id=1, source_target_pairs={{0,3},{1,2},{2,1},{3,0},{4,7},{5,6},{6,5},{7,4},{8,11},{9,10},{10,... | collective-permute-start | bytes 1544 | tf_op jit(solution)/shard_map/ppermute | solution.py:518
  5.3 34.1 %collective-permute-start.20 = (bf16[256]{0:T(256)(128)(2,1)S(1)}, bf16[256]{0:T(256)(128)(2,1)S(1)}, u32[]{:S(2)}, u32[]{:S(2)}) collective-permute-start(bf16[256]{0:T(256)(128)(2,1)S(1)} %get-tuple-element.239), channel_id=1, source_target_pairs={{0,2},{1,3},{2,0},{3,1},{4,6},{5,7},{6,4},{7,5},{8,10},{9,11},{10,... | collective-permute-start | bytes 1544 | tf_op jit(solution)/shard_map/ppermute | solution.py:518
  5.9 34.3 %collective-permute-start.18 = (bf16[256]{0:T(256)(128)(2,1)S(1)}, bf16[256]{0:T(256)(128)(2,1)S(1)}, u32[]{:S(2)}, u32[]{:S(2)}) collective-permute-start(bf16[256]{0:T(256)(128)(2,1)S(1)} %get-tuple-element.239), channel_id=1, source_target_pairs={{0,1},{1,0},{2,3},{3,2},{4,5},{5,4},{6,7},{7,6},{8,9},{9,8},{10,11... | collective-permute-start | bytes 1544 | tf_op jit(solution)/shard_map/ppermute | solution.py:518
  6.8 40.4 %collective-permute-start.10 = (bf16[64,512]{1,0:T(8,128)(2,1)S(1)}, bf16[64,512]{1,0:T(8,128)(2,1)S(1)}, u32[]{:S(2)}, u32[]{:S(2)}) collective-permute-start(bf16[64,512]{1,0:T(8,128)(2,1)S(1)} %get-tuple-element.188), channel_id=1, source_target_pairs={{0,3},{1,2},{2,1},{3,0},{4,7},{5,6},{6,5},{7,4},{8,11},{9,10},{10,... | collective-permute-start | bytes 196616 | tf_op jit(solution)/shard_map/ppermute | solution.py:518
  9.8 36.1 %collective-permute-start.8 = (bf16[64,512]{1,0:T(8,128)(2,1)S(1)}, bf16[64,512]{1,0:T(8,128)(2,1)S(1)}, u32[]{:S(2)}, u32[]{:S(2)}) collective-permute-start(bf16[64,512]{1,0:T(8,128)(2,1)S(1)} %get-tuple-element.188), channel_id=1, source_target_pairs={{0,2},{1,3},{2,0},{3,1},{4,6},{5,7},{6,4},{7,5},{8,10},{9,11},{10,... | collective-permute-start | bytes 196616 | tf_op jit(solution)/shard_map/ppermute | solution.py:518
  40.2 21.8 %collective-permute-start = (bf16[513,192]{1,0:T(8,128)(2,1)S(1)}, bf16[513,192]{1,0:T(8,128)(2,1)S(1)}, u32[]{:S(2)}, u32[]{:S(2)}) collective-permute-start(bf16[513,192]{1,0:T(8,128)(2,1)S(1)} %pad_maximum_fusion.8), channel_id=1, source_target_pairs={{0,1},{1,0},{2,3},{3,2},{4,5},{5,4},{6,7},{7,6},{8,9},{9,8},{10,11... | collective-permute-start | bytes 590984 | tf_op jit(solution)/shard_map/ppermute | solution.py:518
  43.7 16.6 %collective-permute-start.4 = (bf16[513,192]{1,0:T(8,128)(2,1)S(1)}, bf16[513,192]{1,0:T(8,128)(2,1)S(1)}, u32[]{:S(2)}, u32[]{:S(2)}) collective-permute-start(bf16[513,192]{1,0:T(8,128)(2,1)S(1)} %pad_maximum_fusion.8), channel_id=1, source_target_pairs={{0,3},{1,2},{2,1},{3,0},{4,7},{5,6},{6,5},{7,4},{8,11},{9,10},{10,... | collective-permute-start | bytes 590984 | tf_op jit(solution)/shard_map/ppermute | solution.py:518
  47.3 45.3 %collective-permute-start.16 = (bf16[512,256]{1,0:T(8,128)(2,1)S(1)}, bf16[512,256]{1,0:T(8,128)(2,1)}, u32[]{:S(2)}, u32[]{:S(2)}) collective-permute-start(bf16[512,256]{1,0:T(8,128)(2,1)S(1)} %get-tuple-element.128), channel_id=1, source_target_pairs={{0,3},{1,2},{2,1},{3,0},{4,7},{5,6},{6,5},{7,4},{8,11},{9,10},{10,... | collective-permute-start | bytes 786440 | tf_op jit(solution)/shard_map/ppermute | solution.py:518
  50.4 45.7 %collective-permute-start.14 = (bf16[512,256]{1,0:T(8,128)(2,1)S(1)}, bf16[512,256]{1,0:T(8,128)(2,1)}, u32[]{:S(2)}, u32[]{:S(2)}) collective-permute-start(bf16[512,256]{1,0:T(8,128)(2,1)S(1)} %get-tuple-element.128), channel_id=1, source_target_pairs={{0,2},{1,3},{2,0},{3,1},{4,6},{5,7},{6,4},{7,5},{8,10},{9,11},{10,... | collective-permute-start | bytes 786440 | tf_op jit(solution)/shard_map/ppermute | solution.py:518
  58.9 37.1 %collective-permute-start.12 = (bf16[512,256]{1,0:T(8,128)(2,1)S(1)}, bf16[512,256]{1,0:T(8,128)(2,1)}, u32[]{:S(2)}, u32[]{:S(2)}) collective-permute-start(bf16[512,256]{1,0:T(8,128)(2,1)S(1)} %get-tuple-element.128), channel_id=1, source_target_pairs={{0,1},{1,0},{2,3},{3,2},{4,5},{5,4},{6,7},{7,6},{8,9},{9,8},{10,11... | collective-permute-start | bytes 786440 | tf_op jit(solution)/shard_map/ppermute | solution.py:518
  60.3 37.7 %collective-permute-start.28 = (bf16[256,512]{1,0:T(8,128)(2,1)S(1)}, bf16[256,512]{1,0:T(8,128)(2,1)}, u32[]{:S(2)}, u32[]{:S(2)}) collective-permute-start(bf16[256,512]{1,0:T(8,128)(2,1)S(1)} %get-tuple-element.126), channel_id=1, source_target_pairs={{0,3},{1,2},{2,1},{3,0},{4,7},{5,6},{6,5},{7,4},{8,11},{9,10},{10,... | collective-permute-start | bytes 786440 | tf_op jit(solution)/shard_map/ppermute | solution.py:518
  71.8 32.1 %collective-permute-start.26 = (bf16[256,512]{1,0:T(8,128)(2,1)S(1)}, bf16[256,512]{1,0:T(8,128)(2,1)S(1)}, u32[]{:S(2)}, u32[]{:S(2)}) collective-permute-start(bf16[256,512]{1,0:T(8,128)(2,1)S(1)} %get-tuple-element.126), channel_id=1, source_target_pairs={{0,2},{1,3},{2,0},{3,1},{4,6},{5,7},{6,4},{7,5},{8,10},{9,11},{10,... | collective-permute-start | bytes 786440 | tf_op jit(solution)/shard_map/ppermute | solution.py:518
  155.8 103.3 %collective-permute-start.117 = (f32[256]{0:T(256)S(1)}, f32[256]{0:T(256)S(1)}, u32[]{:S(2)}, u32[]{:S(2)}) collective-permute-start(f32[256]{0:T(256)S(1)} %bitcast.101), channel_id=1, source_target_pairs={{0,4},{4,0},{8,12},{12,8},{16,20},{20,16},{24,28},{28,24},{1,5},{5... | collective-permute-start | bytes 3080 | tf_op jit(solution)/shard_map/ppermute | solution.py:522
  156.0 103.7 %collective-permute-start.119 = (f32[256]{0:T(256)S(1)}, f32[256]{0:T(256)S(1)}, u32[]{:S(2)}, u32[]{:S(2)}) collective-permute-start(f32[256]{0:T(256)S(1)} %bitcast.100), channel_id=1, source_target_pairs={{0,4},{4,0},{8,12},{12,8},{16,20},{20,16},{24,28},{28,24},{1,5},{5... | collective-permute-start | bytes 3080 | tf_op jit(solution)/shard_map/ppermute | solution.py:522
  172.4 57.0 %collective-permute-start.81 = (f32[64]{0:T(128)}, f32[64]{0:T(128)S(1)}, u32[]{:S(2)}, u32[]{:S(2)}) collective-permute-start(f32[64]{0:T(128)} %get-tuple-element.219), channel_id=1, source_target_pairs={{0,4},{4,0},{8,12},{12,8},{16,20},{20,16},{24,28},{28,24},{1,5},{5... | collective-permute-start | bytes 776 | tf_op jit(solution)/shard_map/ppermute | solution.py:522
  192.7 31.5 %collective-permute-start.86 = (f32[64]{0:T(128)}, f32[64]{0:T(128)}, u32[]{:S(2)}, u32[]{:S(2)}) collective-permute-start(f32[64]{0:T(128)} %get-tuple-element.231), channel_id=1, source_target_pairs={{0,4},{4,0},{8,12},{12,8},{16,20},{20,16},{24,28},{28,24},{1,5},{5... | collective-permute-start | bytes 776 | tf_op jit(solution)/shard_map/ppermute | solution.py:522
  193.6 33.0 %collective-permute-start.53 = (f32[64]{0:T(128)}, f32[64]{0:T(128)}, u32[]{:S(2)}, u32[]{:S(2)}) collective-permute-start(f32[64]{0:T(128)} %get-tuple-element.232), channel_id=1, source_target_pairs={{0,4},{4,0},{8,12},{12,8},{16,20},{20,16},{24,28},{28,24},{1,5},{5... | collective-permute-start | bytes 776 | tf_op jit(solution)/shard_map/ppermute | solution.py:522
  237.4 25.9 %collective-permute-start.114 = (f32[256]{0:T(256)S(1)}, f32[256]{0:T(256)S(1)}, u32[]{:S(2)}, u32[]{:S(2)}) collective-permute-start(f32[256]{0:T(256)S(1)} %bitcast.102), channel_id=1, source_target_pairs={{0,4},{4,0},{8,12},{12,8},{16,20},{20,16},{24,28},{28,24},{1,5},{5... | collective-permute-start | bytes 3080 | tf_op jit(solution)/shard_map/ppermute | solution.py:522
  258.9 30.4 %collective-permute-start.93 = (bf16[64,512]{1,0:T(8,128)(2,1)}, bf16[64,512]{1,0:T(8,128)(2,1)S(1)}, u32[]{:S(2)}, u32[]{:S(2)}) collective-permute-start(bf16[64,512]{1,0:T(8,128)(2,1)} %slice.611), channel_id=1, source_target_pairs={{0,4},{4,0},{8,12},{12,8},{16,20},{20,16},{24,28},{28,24},{1,5},{5... | collective-permute-start | bytes 196616 | tf_op jit(solution)/shard_map/ppermute | solution.py:522
  263.3 27.6 %collective-permute-start.70 = (bf16[512,64]{1,0:T(8,128)(2,1)}, bf16[512,64]{1,0:T(8,128)(2,1)S(1)}, u32[]{:S(2)}, u32[]{:S(2)}) collective-permute-start(bf16[512,64]{1,0:T(8,128)(2,1)} %get-tuple-element.138), channel_id=1, source_target_pairs={{0,4},{4,0},{8,12},{12,8},{16,20},{20,16},{24,28},{28,24},{1,5},{5... | collective-permute-start | bytes 196616 | tf_op jit(solution)/shard_map/ppermute | solution.py:522
  310.3 51.5 %collective-permute-start.130 = (bf16[256,512]{1,0:T(8,128)(2,1)S(1)}, bf16[256,512]{1,0:T(8,128)(2,1)S(1)}, u32[]{:S(2)}, u32[]{:S(2)}) collective-permute-start(bf16[256,512]{1,0:T(8,128)(2,1)S(1)} %copy-done.27), channel_id=1, source_target_pairs={{0,4},{4,0},{8,12},{12,8},{16,20},{20,16},{24,28},{28,24},{1,5},{5... | collective-permute-start | bytes 786440 | tf_op jit(solution)/shard_map/ppermute | solution.py:522
  316.2 45.8 %collective-permute-start.128 = (bf16[256,512]{1,0:T(8,128)(2,1)S(1)}, bf16[256,512]{1,0:T(8,128)(2,1)S(1)}, u32[]{:S(2)}, u32[]{:S(2)}) collective-permute-start(bf16[256,512]{1,0:T(8,128)(2,1)S(1)} %copy-done.26), channel_id=1, source_target_pairs={{0,4},{4,0},{8,12},{12,8},{16,20},{20,16},{24,28},{28,24},{1,5},{5... | collective-permute-start | bytes 786440 | tf_op jit(solution)/shard_map/ppermute | solution.py:522
  318.7 16.3 %collective-permute-start.78 = (bf16[512,64]{1,0:T(8,128)(2,1)S(1)}, bf16[512,64]{1,0:T(8,128)(2,1)S(1)}, u32[]{:S(2)}, u32[]{:S(2)}) collective-permute-start(bf16[512,64]{1,0:T(8,128)(2,1)S(1)} %get-tuple-element.135), channel_id=1, source_target_pairs={{0,16},{4,20},{8,24},{12,28},{16,0},{20,4},{24,8},{28,12},{1,17},{... | collective-permute-start | bytes 196616 | tf_op jit(solution)/shard_map/ppermute | solution.py:522
  319.9 15.1 %collective-permute-start.77 = (bf16[512,64]{1,0:T(8,128)(2,1)S(1)}, bf16[512,64]{1,0:T(8,128)(2,1)S(1)}, u32[]{:S(2)}, u32[]{:S(2)}) collective-permute-start(bf16[512,64]{1,0:T(8,128)(2,1)S(1)} %get-tuple-element.135), channel_id=1, source_target_pairs={{0,8},{4,12},{8,0},{12,4},{16,24},{20,28},{24,16},{28,20},{1,9},{5... | collective-permute-start | bytes 196616 | tf_op jit(solution)/shard_map/ppermute | solution.py:522
  361.2 22.7 %collective-permute-start.125 = (bf16[256,512]{1,0:T(8,128)(2,1)S(1)}, bf16[256,512]{1,0:T(8,128)(2,1)S(1)}, u32[]{:S(2)}, u32[]{:S(2)}) collective-permute-start(bf16[256,512]{1,0:T(8,128)(2,1)S(1)} %slice.644), channel_id=1, source_target_pairs={{0,4},{4,0},{8,12},{12,8},{16,20},{20,16},{24,28},{28,24},{1,5},{5... | collective-permute-start | bytes 786440 | tf_op jit(solution)/shard_map/ppermute | solution.py:522
  371.6 15.4 %collective-permute-start.131 = (bf16[256,512]{1,0:T(8,128)(2,1)S(1)}, bf16[256,512]{1,0:T(8,128)(2,1)S(1)}, u32[]{:S(2)}, u32[]{:S(2)}) collective-permute-start(bf16[256,512]{1,0:T(8,128)(2,1)S(1)} %slice_add_fusion), channel_id=1, source_target_pairs={{0,3},{1,2},{2,1},{3,0},{4,7},{5,6},{6,5},{7,4},{8,11},{9,10},{10,... | collective-permute-start | bytes 786440 | tf_op jit(solution)/shard_map/ppermute | solution.py:518
  375.7 16.6 %collective-permute-start.129 = (bf16[256,512]{1,0:T(8,128)(2,1)S(1)}, bf16[256,512]{1,0:T(8,128)(2,1)S(1)}, u32[]{:S(2)}, u32[]{:S(2)}) collective-permute-start(bf16[256,512]{1,0:T(8,128)(2,1)S(1)} %slice_add_fusion.1), channel_id=1, source_target_pairs={{0,2},{1,3},{2,0},{3,1},{4,6},{5,7},{6,4},{7,5},{8,10},{9,11},{10,... | collective-permute-start | bytes 786440 | tf_op jit(solution)/shard_map/ppermute | solution.py:518
  384.0 35.7 %collective-permute-start.111 = (bf16[512,256]{1,0:T(8,128)(2,1)S(1)}, bf16[512,256]{1,0:T(8,128)(2,1)S(1)}, u32[]{:S(2)}, u32[]{:S(2)}) collective-permute-start(bf16[512,256]{1,0:T(8,128)(2,1)S(1)} %add_convert_fusion.3), channel_id=1, source_target_pairs={{0,16},{4,20},{8,24},{12,28},{16,0},{20,4},{24,8},{28,12},{1,17},{... | collective-permute-start | bytes 786440 | tf_op jit(solution)/shard_map/ppermute | solution.py:522
  387.0 32.7 %collective-permute-start.110 = (bf16[512,256]{1,0:T(8,128)(2,1)S(1)}, bf16[512,256]{1,0:T(8,128)(2,1)S(1)}, u32[]{:S(2)}, u32[]{:S(2)}) collective-permute-start(bf16[512,256]{1,0:T(8,128)(2,1)S(1)} %add_convert_fusion.3), channel_id=1, source_target_pairs={{0,8},{4,12},{8,0},{12,4},{16,24},{20,28},{24,16},{28,20},{1,9},{5... | collective-permute-start | bytes 786440 | tf_op jit(solution)/shard_map/ppermute | solution.py:522
  392.5 28.2 %collective-permute-start.134 = (bf16[256,512]{1,0:T(8,128)(2,1)S(1)}, bf16[256,512]{1,0:T(8,128)(2,1)S(1)}, u32[]{:S(2)}, u32[]{:S(2)}) collective-permute-start(bf16[256,512]{1,0:T(8,128)(2,1)S(1)} %add_convert_fusion.1), channel_id=1, source_target_pairs={{0,24},{4,28},{8,16},{12,20},{16,8},{20,12},{24,0},{28,4},{1,25},{... | collective-permute-start | bytes 786440 | tf_op jit(solution)/shard_map/ppermute | solution.py:522
  394.6 34.9 %collective-permute-start.133 = (bf16[256,512]{1,0:T(8,128)(2,1)S(1)}, bf16[256,512]{1,0:T(8,128)(2,1)S(1)}, u32[]{:S(2)}, u32[]{:S(2)}) collective-permute-start(bf16[256,512]{1,0:T(8,128)(2,1)S(1)} %add_convert_fusion.1), channel_id=1, source_target_pairs={{0,16},{4,20},{8,24},{12,28},{16,0},{20,4},{24,8},{28,12},{1,17},{... | collective-permute-start | bytes 786440 | tf_op jit(solution)/shard_map/ppermute | solution.py:522
  395.3 34.1 %collective-permute-start.132 = (bf16[256,512]{1,0:T(8,128)(2,1)S(1)}, bf16[256,512]{1,0:T(8,128)(2,1)S(1)}, u32[]{:S(2)}, u32[]{:S(2)}) collective-permute-start(bf16[256,512]{1,0:T(8,128)(2,1)S(1)} %add_convert_fusion.1), channel_id=1, source_target_pairs={{0,8},{4,12},{8,0},{12,4},{16,24},{20,28},{24,16},{28,20},{1,9},{5... | collective-permute-start | bytes 786440 | tf_op jit(solution)/shard_map/ppermute | solution.py:522
  (149 other events, 1446.3 us)
